TPU v7x, 128 devices: a whole 4x4x4 slice. The times are simulated.
128 devices in a mesh: nodes: 8 (over x, core), feat: 16 (over z, y).
Axes of the slice: x: 4, y: 4, z: 4, core: 2. Of those that a mesh axis runs over, the one named last changes fastest.
Arguments:
- node_states: float32 [2, 128, 16384], P(None, 'feat', 'nodes'), may hold values from -6 to 6
- weights: bfloat16 [2, 2, 128, 128], replicated, may hold values from -0.5 to 0.5
- adj_tiles: bfloat16 [128, 4, 128, 128], P('nodes'), may hold values from -0.25 to 0.25
- tile_source: int32 [128, 4], P('nodes'), may hold values from 0 to 31
- tile_count: int32 [128], P('nodes'), may hold values from 1 to 4, as said below
- send_rows: int32 [8, 8, 256], P('nodes'), may hold values from 0 to 2047
- send_count: int32 [8, 8], P('nodes'), may hold values from 1 to 256, as said below
- out_grads: float32 [2, 128, 16384], P(None, 'feat', 'nodes'), may hold values from -6 to 6
Outputs:
- outputs: float32 [2, 128, 16384], P(None, 'feat', 'nodes')
- state_grads: float32 [2, 128, 16384], P(None, 'feat', 'nodes')
- weight_grads: float32 [2, 2, 128, 128], P(None, None, None, 'feat')
Inputs may be any that keep to these rules, and one draw needn't show every extreme that they name: `tile_count`: live slots of a destination block; some block holds 4. `send_count`: rows a sender sends to a receiver; every device sends 256 to one receiver and receives 256 from one sender.
All inputs are finite; a program needn't handle non-finite values.
Results may differ from a plain program's by a relative error of at most 0.015.
Values may be sent and summed in bfloat16 or wider, within the bound.
A program may use at most 64 MiB of HBM per device.

v0:
```python
import jax
import jax.numpy as jnp
from jax import lax
from jax.sharding import PartitionSpec as P

TILE = 128


EPS = 1e-05


def normalize(states, total_width):
    sums = lax.psum((jnp.sum(states, axis=0), jnp.sum(states * states, axis=0)), "feat")
    center = sums[0] / total_width
    spread = sums[1] / total_width - center * center
    inverse = lax.rsqrt(spread + EPS)
    return ((states - center) * inverse, inverse)


def aggregate(source, sources, values):
    width = source.shape[0]
    blocks = source.reshape(width, -1, TILE)[:, sources]
    result = jnp.einsum("jtkc,tkrc->jtr", blocks, values, preferred_element_type=jnp.float32)
    return result.reshape(width, -1)


def fetch_rim(outgoing):
    return lax.all_to_all(outgoing, "nodes", split_axis=1, concat_axis=1, tiled=True)


def own_columns(weight, width):
    start = lax.axis_index("feat") * width
    return lax.dynamic_slice_in_dim(weight, start, width, 1)


def forward_branch(states, weight, graph):
    values, sources, send_index, send_live = graph
    width, rows = states.shape
    total_width = weight.shape[0]
    normed, inverse = normalize(states, total_width)
    activ = jax.nn.silu(normed).astype(jnp.bfloat16)
    full_act = lax.all_gather(activ, "feat", axis=0, tiled=True)
    columns = own_columns(weight, width)
    mixed = lax.dot_general(
        columns, full_act, (((0,), (0,)), ((), ())), preferred_element_type=jnp.float32
    ).astype(jnp.bfloat16)
    outgoing = jnp.where(
        send_live, jnp.take(mixed, send_index, axis=1), jnp.zeros((), jnp.bfloat16)
    )
    sent_cols = outgoing.shape[1]
    halo_rows = (sent_cols + TILE - 1) // TILE * TILE
    rim_pad = jnp.zeros((width, halo_rows - sent_cols), jnp.bfloat16)
    incoming = fetch_rim(outgoing)
    result = aggregate(jnp.concatenate([mixed, incoming, rim_pad], axis=1), sources, values)
    return (result, (normed, inverse, full_act, incoming))


def backward_branch(grad, weight, graph, saved):
    values, sources, send_index, send_live = graph
    normed, inverse, full_act, incoming = saved
    width, rows = grad.shape
    total_width = weight.shape[0]
    sent_cols = send_index.shape[0]
    halo_rows = (sent_cols + TILE - 1) // TILE * TILE
    source_tiles = (rows + halo_rows) // TILE
    grad_low = grad.astype(jnp.bfloat16).reshape(width, -1, TILE)
    terms = jnp.einsum("jtr,tkrc->jtkc", grad_low, values, preferred_element_type=jnp.float32)
    source = (
        jnp.zeros((width, source_tiles, TILE), jnp.float32)
        .at[:, sources]
        .add(terms)
        .reshape(width, -1)
    )
    rim = source[:, rows : rows + sent_cols].astype(jnp.bfloat16)
    returned = lax.all_to_all(rim, "nodes", split_axis=1, concat_axis=1, tiled=True)
    returned = jnp.where(send_live, returned, jnp.zeros((), jnp.bfloat16)).astype(jnp.float32)
    grad_mixed = source[:, :rows].at[:, send_index].add(returned).astype(jnp.bfloat16)
    weight_part = lax.dot_general(
        full_act, grad_mixed, (((1,), (1,)), ((), ())), preferred_element_type=jnp.float32
    )
    columns = own_columns(weight, width)
    grad_act = lax.psum_scatter(
        jnp.dot(columns, grad_mixed, preferred_element_type=jnp.float32).astype(jnp.bfloat16),
        "feat",
        scatter_dimension=0,
        tiled=True,
    ).astype(jnp.float32)
    gate = jax.nn.sigmoid(normed)
    grad_norm = grad_act * gate * (1.0 + normed * (1.0 - gate))
    sums = lax.psum((jnp.sum(grad_norm, axis=0), jnp.sum(grad_norm * normed, axis=0)), "feat")
    grad_states = inverse * (grad_norm - sums[0] / total_width - normed * sums[1] / total_width)
    return (grad_states, weight_part)


def body(
    node_states, weights, adj_tiles, tile_source, tile_count, send_rows, send_count, out_grads
):
    slots = send_rows.shape[2]
    send_index = send_rows[0].reshape(-1)
    send_live = (jnp.arange(slots, dtype=jnp.int32)[None, :] < send_count[0][:, None]).reshape(
        1, -1
    )
    depth = adj_tiles.shape[1]
    keep = jnp.arange(depth, dtype=jnp.int32)[None, :] < tile_count[:, None]
    values = jnp.where(keep[:, :, None, None], adj_tiles, jnp.zeros((), jnp.bfloat16))
    graph = (values, tile_source, send_index, send_live)
    layers = weights.shape[0]
    first, second = (node_states[0], node_states[1])
    rims = []
    for layer in range(layers):
        lift, saved_first = forward_branch(second, weights[layer, 0], graph)
        first = first + lift
        lift, saved_second = forward_branch(first, weights[layer, 1], graph)
        second = second + lift
        rims.append((saved_first[3], saved_second[3]))
    outputs = jnp.stack([first, second])
    grad_first, grad_second = (out_grads[0], out_grads[1])
    collected = []
    for layer in range(layers - 1, -1, -1):
        lift, saved = forward_branch(first, weights[layer, 1], graph)
        second = second - lift
        grad_states, part_second = backward_branch(grad_second, weights[layer, 1], graph, saved)
        grad_first = grad_first + grad_states
        lift, saved = forward_branch(second, weights[layer, 0], graph)
        first = first - lift
        grad_states, part_first = backward_branch(grad_first, weights[layer, 0], graph, saved)
        grad_second = grad_second + grad_states
        part_first, part_second = lax.psum((part_first, part_second), "nodes")
        collected.append(jnp.stack([part_first, part_second]))
    weight_grads = jnp.stack(collected[::-1])
    return (outputs, jnp.stack([grad_first, grad_second]), weight_grads)


def solution(mesh):
    return jax.shard_map(
        body,
        mesh=mesh,
        in_specs=(
            P(None, "feat", "nodes"),
            P(),
            P("nodes", None, None, None),
            P("nodes", None),
            P("nodes"),
            P("nodes", None, None),
            P("nodes", None),
            P(None, "feat", "nodes"),
        ),
        out_specs=(P(None, "feat", "nodes"), P(None, "feat", "nodes"), P(None, None, None, "feat")),
        check_vma=False,
    )
```

profile of v0, /device:TPU:1, one launch (start us, length us, event | category | flops | bytes accessed | tf_op | source)
XLA Modules:
  0.0 1212.0 jit_solution(12980790530727956138)
XLA Ops:
  11.3 62.5 %all-reduce.11 = (f32[2048]{0:T(1024)S(1)}, f32[2048]{0:T(1024)S(1)}) all-reduce(f32[2048]{0:T(1024)S(1)} %fusion.26, f32[2048]{0:T(1024)S(1)} %slice_reduce_fusion), channel_id=1, replica_groups=mesh['nodes'=8,'feat'=16] {'feat'}, use_global_device_ids=true, to_apply=%region_3.4 | all-reduce | flops 4096 | bytes 32768 | tf_op jit(solution)/shard_map/psum | solution.py:13
  74.7 16.0 %all_gather.22 = bf16[128,2048]{1,0:T(8,128)(2,1)S(1)} all-gather(bf16[8,2048]{1,0:T(8,128)(2,1)S(1)} %multiply_convert_fusion.6), channel_id=1, replica_groups=mesh['nodes'=8,'feat'=16] {'feat'}, dimensions={0}, use_global_device_ids=true | all-gather | bytes 557056 | tf_op jit(solution)/shard_map/all_gather | solution.py:42
  99.8 24.3 %all-to-all-start = ((bf16[8,8,256]{2,0,1:T(8,128)(2,1)}), bf16[8,8,256]{2,0,1:T(8,128)(2,1)S(1)}, u32[]{:S(2)}, u32[]{:S(2)}) async-start(bf16[8,8,256]{2,0,1:T(8,128)(2,1)} %copy.79), calls=%async_computation | async-start | bytes 65536 | tf_op jit(solution)/shard_map/all_to_all | solution.py:28
  136.7 57.9 %all-reduce.10 = (f32[2048]{0:T(1024)S(1)}, f32[2048]{0:T(1024)S(1)}) all-reduce(f32[2048]{0:T(1024)S(1)} %get-tuple-element.23, f32[2048]{0:T(1024)S(1)} %get-tuple-element.22), channel_id=1, replica_groups=mesh['nodes'=8,'feat'=16] {'feat'}, use_global_device_ids=true, to_apply=%region_7.9 | all-reduce | flops 4096 | bytes 32768 | tf_op jit(solution)/shard_map/psum | solution.py:13
  194.6 16.0 %all_gather.23 = bf16[128,2048]{1,0:T(8,128)(2,1)S(1)} all-gather(bf16[8,2048]{1,0:T(8,128)(2,1)S(1)} %multiply_convert_fusion.5), channel_id=1, replica_groups=mesh['nodes'=8,'feat'=16] {'feat'}, dimensions={0}, use_global_device_ids=true | all-gather | bytes 557056 | tf_op jit(solution)/shard_map/all_gather | solution.py:42
  220.0 23.9 %all-to-all-start.1 = ((bf16[8,8,256]{2,0,1:T(8,128)(2,1)}), bf16[8,8,256]{2,0,1:T(8,128)(2,1)S(1)}, u32[]{:S(2)}, u32[]{:S(2)}) async-start(bf16[8,8,256]{2,0,1:T(8,128)(2,1)} %copy.84), calls=%async_computation.1 | async-start | bytes 65536 | tf_op jit(solution)/shard_map/all_to_all | solution.py:28
  245.6 11.9 scatter_custom_fusion.1
  260.5 58.0 %all-reduce.9 = (f32[2048]{0:T(1024)S(1)}, f32[2048]{0:T(1024)S(1)}) all-reduce(f32[2048]{0:T(1024)S(1)} %get-tuple-element.21, f32[2048]{0:T(1024)S(1)} %get-tuple-element.20), channel_id=1, replica_groups=mesh['nodes'=8,'feat'=16] {'feat'}, use_global_device_ids=true, to_apply=%region_11.13 | all-reduce | flops 4096 | bytes 32768 | tf_op jit(solution)/shard_map/psum | solution.py:13
  318.5 16.0 %all_gather.24 = bf16[128,2048]{1,0:T(8,128)(2,1)S(1)} all-gather(bf16[8,2048]{1,0:T(8,128)(2,1)S(1)} %multiply_convert_fusion.4), channel_id=1, replica_groups=mesh['nodes'=8,'feat'=16] {'feat'}, dimensions={0}, use_global_device_ids=true | all-gather | bytes 557056 | tf_op jit(solution)/shard_map/all_gather | solution.py:42
  343.5 23.9 %all-to-all-start.2 = ((bf16[8,8,256]{2,0,1:T(8,128)(2,1)}), bf16[8,8,256]{2,0,1:T(8,128)(2,1)S(1)}, u32[]{:S(2)}, u32[]{:S(2)}) async-start(bf16[8,8,256]{2,0,1:T(8,128)(2,1)} %copy.88), calls=%async_computation.2 | async-start | bytes 65536 | tf_op jit(solution)/shard_map/all_to_all | solution.py:28
  375.8 58.0 %all-reduce.8 = (f32[2048]{0:T(1024)S(1)}, f32[2048]{0:T(1024)S(1)}) all-reduce(f32[2048]{0:T(1024)S(1)} %bitcast.364, f32[2048]{0:T(1024)S(1)} %bitcast.363), channel_id=1, replica_groups=mesh['nodes'=8,'feat'=16] {'feat'}, use_global_device_ids=true, to_apply=%region_15.17 | all-reduce | flops 4096 | bytes 32768 | tf_op jit(solution)/shard_map/psum | solution.py:13
  433.8 21.4 %all-reduce.18.cloned.1.call-done = bf16[128,2048]{1,0:T(8,128)(2,1)} async-done(((bf16[128,2048]{1,0:T(8,128)(2,1)}), bf16[128,2048]{1,0:T(8,128)(2,1)}) %all-reduce.18.cloned.1.call-update) | async-done | bytes 524304
  456.1 17.5 %all_gather.25 = bf16[128,2048]{1,0:T(8,128)(2,1)S(1)} all-gather(bf16[8,2048]{1,0:T(8,128)(2,1)S(1)} %multiply_convert_fusion.3), channel_id=1, replica_groups=mesh['nodes'=8,'feat'=16] {'feat'}, dimensions={0}, use_global_device_ids=true | all-gather | bytes 557056 | tf_op jit(solution)/shard_map/all_gather | solution.py:42
  481.9 16.6 %all_to_all.103 = bf16[8,8,256]{2,0,1:T(8,128)(2,1)S(1)} all-to-all(bf16[8,8,256]{2,0,1:T(8,128)(2,1)S(1)} %copy.92), channel_id=1, replica_groups=mesh['nodes'=8,'feat'=16] {'nodes'}, dimensions={1} | all-to-all | bytes 65536 | tf_op jit(solution)/shard_map/all_to_all | solution.py:28
  502.8 57.9 %all-reduce.7 = (f32[2048]{0:T(1024)S(1)}, f32[2048]{0:T(1024)S(1)}, f32[2048]{0:T(1024)S(1)}, f32[2048]{0:T(1024)S(1)}) all-reduce(f32[2048]{0:T(1024)S(1)} %bitcast.358, f32[2048]{0:T(1024)S(1)} %bitcast.357, f32[2048]{0:T(1024)S(1)} %get-tuple-element.7, f32[2048]{0:T(1024)S(1)} %get-tuple-element.6), channel_id=1, replica_groups=mesh['nodes'=8,'feat'=16] {'feat'}, use_global_device_ids=true, to_apply=%region_26.28 | all-reduce | flops 8192 | bytes 65536 | tf_op jit(solution)/shard_map/psum | solution.py:13
  566.2 18.2 %all-to-all-start.6 = ((bf16[8,8,256]{2,0,1:T(8,128)(2,1)}), bf16[8,8,256]{2,0,1:T(8,128)(2,1)S(1)}, u32[]{:S(2)}, u32[]{:S(2)}) async-start(bf16[8,8,256]{2,0,1:T(8,128)(2,1)} %bitcast.90), calls=%async_computation.6 | async-start | bytes 65536 | tf_op jit(solution)/shard_map/all_to_all | solution.py:75
  604.6 78.6 %all-reduce.20.cloned.1.call-done = bf16[128,2048]{1,0:T(8,128)(2,1)} async-done(((bf16[128,2048]{1,0:T(8,128)(2,1)}), bf16[128,2048]{1,0:T(8,128)(2,1)}) %all-reduce.20.cloned.1.call-update) | async-done | bytes 524304
  684.1 17.5 %all_gather.26 = bf16[128,2048]{1,0:T(8,128)(2,1)S(1)} all-gather(bf16[8,2048]{1,0:T(8,128)(2,1)S(1)} %multiply_convert_fusion.2), channel_id=1, replica_groups=mesh['nodes'=8,'feat'=16] {'feat'}, dimensions={0}, use_global_device_ids=true | all-gather | bytes 557056 | tf_op jit(solution)/shard_map/all_gather | solution.py:42
  716.4 16.6 %all_to_all.104 = bf16[8,8,256]{2,0,1:T(8,128)(2,1)S(1)} all-to-all(bf16[8,8,256]{2,0,1:T(8,128)(2,1)S(1)} %copy.98), channel_id=1, replica_groups=mesh['nodes'=8,'feat'=16] {'nodes'}, dimensions={1} | all-to-all | bytes 65536 | tf_op jit(solution)/shard_map/all_to_all | solution.py:28
  736.6 57.9 %all-reduce.6 = (f32[2048]{0:T(1024)}, f32[2048]{0:T(1024)}, f32[2048]{0:T(1024)S(1)}, f32[2048]{0:T(1024)S(1)}) all-reduce(f32[2048]{0:T(1024)S(1)} %bitcast.366, f32[2048]{0:T(1024)S(1)} %bitcast.365, f32[2048]{0:T(1024)S(1)} %get-tuple-element.5, f32[2048]{0:T(1024)S(1)} %get-tuple-element.4), channel_id=1, replica_groups=mesh['nodes'=8,'feat'=16] {'feat'}, use_global_device_ids=true, to_apply=%region_30.32 | all-reduce | flops 8192 | bytes 65536 | tf_op jit(solution)/shard_map/psum | solution.py:13
  800.0 18.2 %all-to-all-start.7 = ((bf16[8,8,256]{2,0,1:T(8,128)(2,1)}), bf16[8,8,256]{2,0,1:T(8,128)(2,1)S(1)}, u32[]{:S(2)}, u32[]{:S(2)}) async-start(bf16[8,8,256]{2,0,1:T(8,128)(2,1)} %bitcast.99), calls=%async_computation.7 | async-start | bytes 65536 | tf_op jit(solution)/shard_map/all_to_all | solution.py:75
  825.4 12.3 %scatter_custom_fusion.5 = f32[8,2048]{0,1:T(8,128)S(1)} fusion(f32[8,2048]{0,1:T(8,128)S(1)} %copy.123, s32[2048]{0:T(1024)} %bitcast.361, bf16[8,2048]{0,1:T(8,128)(2,1)S(1)} %bitcast_select_fusion.2), kind=kCustom, calls=%fused_computation.37 | custom fusion | flops 32768 | bytes 589824 | tf_op jit(solution)/shard_map/scatter-add | solution.py:77
  840.5 77.0 %all-reduce.22.cloned.1.call-done = bf16[128,2048]{1,0:T(8,128)(2,1)} async-done(((bf16[128,2048]{1,0:T(8,128)(2,1)}), bf16[128,2048]{1,0:T(8,128)(2,1)}) %all-reduce.22.cloned.1.call-update) | async-done | bytes 524304
  918.4 17.5 %all_gather.27 = bf16[128,2048]{1,0:T(8,128)(2,1)S(1)} all-gather(bf16[8,2048]{1,0:T(8,128)(2,1)S(1)} %multiply_convert_fusion.1), channel_id=1, replica_groups=mesh['nodes'=8,'feat'=16] {'feat'}, dimensions={0}, use_global_device_ids=true | all-gather | bytes 557056 | tf_op jit(solution)/shard_map/all_gather | solution.py:42
  944.9 12.1 all-to-all-start.8
  964.8 57.9 %all-reduce.5 = (f32[2048]{0:T(1024)S(1)}, f32[2048]{0:T(1024)S(1)}, f32[2048]{0:T(1024)S(1)}, f32[2048]{0:T(1024)S(1)}) all-reduce(f32[2048]{0:T(1024)S(1)} %bitcast.368, f32[2048]{0:T(1024)S(1)} %bitcast.367, f32[2048]{0:T(1024)S(1)} %get-tuple-element.11, ...), channel_id=1, replica_groups=mesh['nodes'=8,'feat'=16] {'feat'}, use_global_device_ids=true, to_apply=%region_48.50 | all-reduce | flops 8192 | bytes 65536 | tf_op jit(solution)/shard_map/psum | solution.py:13
  1029.1 18.2 %all-to-all-start.9 = ((bf16[8,8,256]{2,0,1:T(8,128)(2,1)}), bf16[8,8,256]{2,0,1:T(8,128)(2,1)S(1)}, u32[]{:S(2)}, u32[]{:S(2)}) async-start(bf16[8,8,256]{2,0,1:T(8,128)(2,1)} %bitcast.122), calls=%async_computation.9 | async-start | bytes 65536 | tf_op jit(solution)/shard_map/all_to_all | solution.py:75
  1052.6 12.0 scatter_custom_fusion.7
  1065.9 16.3 %all_gather.28 = bf16[128,2048]{1,0:T(8,128)(2,1)S(1)} all-gather(bf16[8,2048]{1,0:T(8,128)(2,1)S(1)} %get-tuple-element.50), channel_id=1, replica_groups=mesh['nodes'=8,'feat'=16] {'feat'}, dimensions={0}, use_global_device_ids=true | all-gather | bytes 557056 | tf_op jit(solution)/shard_map/all_gather | solution.py:42
  1082.5 25.9 %all-reduce.12 = (f32[1,128,8]{1,2,0:T(8,128)S(1)}, f32[1,128,8]{1,2,0:T(8,128)S(1)}, f32[1,128,8]{1,2,0:T(8,128)S(1)}, f32[1,128,8]{1,2,0:T(8,128)S(1)}) all-reduce(f32[1,128,8]{1,2,0:T(8,128)S(1)} %convolution_bitcast_fusion, f32[1,128,8]{1,2,0:T(8,128)S(1)} %copy-done.35, ...), channel_id=1, replica_groups=mesh['nodes'=8,'feat'=16] {'nodes'}, use_global_device_ids=true, to_apply=%region_59.61 | all-reduce | flops 4096 | bytes 32768 | tf_op jit(solution)/shard_map/psum | solution.py:128
  1109.0 35.8 %all-reduce.24.cloned.1.call-done = bf16[128,2048]{1,0:T(8,128)(2,1)} async-done(((bf16[128,2048]{1,0:T(8,128)(2,1)}), bf16[128,2048]{1,0:T(8,128)(2,1)}) %all-reduce.24.cloned.1.call-update) | async-done | bytes 524304
  1145.6 58.3 %all-reduce.4 = (f32[2048]{0:T(1024)S(1)}, f32[2048]{0:T(1024)S(1)}) all-reduce(f32[2048]{0:T(1024)S(1)} %get-tuple-element.9, f32[2048]{0:T(1024)S(1)} %get-tuple-element.8), channel_id=1, replica_groups=mesh['nodes'=8,'feat'=16] {'feat'}, use_global_device_ids=true, to_apply=%region_55.57 | all-reduce | flops 4096 | bytes 32768 | tf_op jit(solution)/shard_map/psum | solution.py:90
  (250 shorter events, 164.7 us)
Async XLA Ops:
  7.9 703.8 %copy-start.23 = (pred[2048]{0:T(1024)(128)(4,1)}, pred[2048]{0:T(1024)(128)(4,1)S(1)}, u32[]{:S(2)}) copy-start(pred[2048]{0:T(1024)(128)(4,1)S(1)} %compare_and_fusion) | copy-start | bytes 6148
  8.8 115.3 %copy-start.46 = (s32[16]{0:T(128)S(1)}, s32[16]{0:T(128)}, u32[]{:S(2)}) copy-start(s32[16]{0:T(128)} %param.14) | copy-start | bytes 196
  8.8 115.3 %copy-start.45 = (s32[16,4]{0,1:T(4,128)S(1)}, s32[16,4]{0,1:T(4,128)}, u32[]{:S(2)}) copy-start(s32[16,4]{0,1:T(4,128)} %param.13) | copy-start | bytes 772
  9.7 114.6 %copy-start.21 = (f32[2,8,2048]{2,1,0:T(8,128)S(1)}, f32[2,8,2048]{2,1,0:T(8,128)}, u32[]{:S(2)}) copy-start(f32[2,8,2048]{2,1,0:T(8,128)} %param.17) | copy-start | bytes 393220
  10.5 701.2 %copy-start.9 = (pred[2048]{0:T(1024)(128)(4,1)}, pred[2048]{0:T(1024)(128)(4,1)S(1)}, u32[]{:S(2)}) copy-start(pred[2048]{0:T(1024)(128)(4,1)S(1)} %lt.92) | copy-start | bytes 6148
  11.3 115.0 %copy-start.7 = (bf16[1,1,128,128]{3,2,1,0:T(8,128)(2,1)}, bf16[1,1,128,128]{3,2,1,0:T(8,128)(2,1)S(1)}, u32[]{:S(2)}) copy-start(bf16[1,1,128,128]{3,2,1,0:T(8,128)(2,1)S(1)} %get-tuple-element.63) | copy-start | bytes 98308
  11.3 199.3 %copy-start.5 = (bf16[1,1,128,128]{3,2,1,0:T(8,128)(2,1)}, bf16[1,1,128,128]{3,2,1,0:T(8,128)(2,1)S(1)}, u32[]{:S(2)}) copy-start(bf16[1,1,128,128]{3,2,1,0:T(8,128)(2,1)S(1)} %get-tuple-element.64) | copy-start | bytes 98308
  99.8 30.0 %all-to-all-start = ((bf16[8,8,256]{2,0,1:T(8,128)(2,1)}), bf16[8,8,256]{2,0,1:T(8,128)(2,1)S(1)}, u32[]{:S(2)}, u32[]{:S(2)}) async-start(bf16[8,8,256]{2,0,1:T(8,128)(2,1)} %copy.79), calls=%async_computation | async-start | bytes 65536 | tf_op jit(solution)/shard_map/all_to_all | solution.py:28
  124.1 609.6 %copy-start.43 = (pred[16,4]{1,0:T(8,128)(4,1)}, pred[16,4]{1,0:T(8,128)(4,1)S(1)}, u32[]{:S(2)}) copy-start(pred[16,4]{1,0:T(8,128)(4,1)S(1)} %iota_compare_fusion.1) | copy-start | bytes 196
  129.8 87.6 %all-to-all-start.4 = ((bf16[8,8,256]{2,0,1:T(8,128)(2,1)}), bf16[8,8,256]{2,0,1:T(8,128)(2,1)S(1)}, u32[]{:S(2)}, u32[]{:S(2)}) async-start(bf16[8,8,256]{2,0,1:T(8,128)(2,1)} %bitcast.64), calls=%async_computation.4 | async-start | bytes 65536 | tf_op jit(solution)/shard_map/all_to_all | solution.py:75
  220.0 37.5 %all-to-all-start.1 = ((bf16[8,8,256]{2,0,1:T(8,128)(2,1)}), bf16[8,8,256]{2,0,1:T(8,128)(2,1)S(1)}, u32[]{:S(2)}, u32[]{:S(2)}) async-start(bf16[8,8,256]{2,0,1:T(8,128)(2,1)} %copy.84), calls=%async_computation.1 | async-start | bytes 65536 | tf_op jit(solution)/shard_map/all_to_all | solution.py:28
  243.9 347.5 %copy-start.40 = (s32[2048,1]{0,1:T(1,128)}, s32[2048,1]{0,1:T(1,128)S(1)}, u32[]{:S(2)}) copy-start(s32[2048,1]{0,1:T(1,128)S(1)} %compare_select_fusion) | copy-start | bytes 24580
  343.5 28.6 %all-to-all-start.2 = ((bf16[8,8,256]{2,0,1:T(8,128)(2,1)}), bf16[8,8,256]{2,0,1:T(8,128)(2,1)S(1)}, u32[]{:S(2)}, u32[]{:S(2)}) async-start(bf16[8,8,256]{2,0,1:T(8,128)(2,1)} %copy.88), calls=%async_computation.2 | async-start | bytes 65536 | tf_op jit(solution)/shard_map/all_to_all | solution.py:28
  367.4 87.7 %all-reduce.18.cloned.1.call-start = ((), (), s32[]{:S(2)}) async-start(), calls=%async_computation.10 | async-start | bytes 1048576
  433.7 127.0 %copy-start.17 = (f32[2048]{0:T(1024)}, f32[2048]{0:T(1024)S(1)}, u32[]{:S(2)}) copy-start(f32[2048]{0:T(1024)S(1)} %get-tuple-element.71) | copy-start | bytes 24580
  433.7 127.0 %copy-start.19 = (f32[2048]{0:T(1024)}, f32[2048]{0:T(1024)S(1)}, u32[]{:S(2)}) copy-start(f32[2048]{0:T(1024)S(1)} %get-tuple-element.72) | copy-start | bytes 24580
  456.0 104.7 %copy-start.2 = (f32[8,2048]{1,0:T(8,128)}, f32[8,2048]{1,0:T(8,128)S(1)}, u32[]{:S(2)}) copy-start(f32[8,2048]{1,0:T(8,128)S(1)} %get-tuple-element.54) | copy-start | bytes 196612
  566.2 22.9 %all-to-all-start.6 = ((bf16[8,8,256]{2,0,1:T(8,128)(2,1)}), bf16[8,8,256]{2,0,1:T(8,128)(2,1)S(1)}, u32[]{:S(2)}, u32[]{:S(2)}) async-start(bf16[8,8,256]{2,0,1:T(8,128)(2,1)} %bitcast.90), calls=%async_computation.6 | async-start | bytes 65536 | tf_op jit(solution)/shard_map/all_to_all | solution.py:75
  584.3 98.9 %all-reduce.20.cloned.1.call-start = ((), (), s32[]{:S(2)}) async-start(), calls=%async_computation.11 | async-start | bytes 1048576
  604.6 128.4 %copy-start.11 = (f32[2048]{0:T(1024)}, f32[2048]{0:T(1024)S(1)}, u32[]{:S(2)}) copy-start(f32[2048]{0:T(1024)S(1)} %get-tuple-element.69) | copy-start | bytes 24580
  604.6 128.4 %copy-start.14 = (f32[2048]{0:T(1024)}, f32[2048]{0:T(1024)S(1)}, u32[]{:S(2)}) copy-start(f32[2048]{0:T(1024)S(1)} %get-tuple-element.70) | copy-start | bytes 24580
  684.1 110.4 %copy-start = (f32[8,2048]{1,0:T(8,128)}, f32[8,2048]{1,0:T(8,128)S(1)}, u32[]{:S(2)}) copy-start(f32[8,2048]{1,0:T(8,128)S(1)} %get-tuple-element.53) | copy-start | bytes 196612
  800.0 22.9 %all-to-all-start.7 = ((bf16[8,8,256]{2,0,1:T(8,128)(2,1)}), bf16[8,8,256]{2,0,1:T(8,128)(2,1)S(1)}, u32[]{:S(2)}, u32[]{:S(2)}) async-start(bf16[8,8,256]{2,0,1:T(8,128)(2,1)} %bitcast.99), calls=%async_computation.7 | async-start | bytes 65536 | tf_op jit(solution)/shard_map/all_to_all | solution.py:75
  818.2 99.3 %all-reduce.22.cloned.1.call-start = ((), (), s32[]{:S(2)}) async-start(), calls=%async_computation.12 | async-start | bytes 1048576
  838.9 103.8 %copy-start.24 = (pred[2048]{0:T(1024)(128)(4,1)S(1)}, pred[2048]{0:T(1024)(128)(4,1)}, u32[]{:S(2)}) copy-start(pred[2048]{0:T(1024)(128)(4,1)} %copy-done.23) | copy-start | bytes 6148
  944.9 16.8 %all-to-all-start.8 = ((bf16[8,8,256]{2,0,1:T(8,128)(2,1)}), bf16[8,8,256]{2,0,1:T(8,128)(2,1)S(1)}, u32[]{:S(2)}, u32[]{:S(2)}) async-start(bf16[8,8,256]{2,0,1:T(8,128)(2,1)} %copy.106), calls=%async_computation.8 | async-start | bytes 65536 | tf_op jit(solution)/shard_map/all_to_all | solution.py:28
  1029.1 22.9 %all-to-all-start.9 = ((bf16[8,8,256]{2,0,1:T(8,128)(2,1)}), bf16[8,8,256]{2,0,1:T(8,128)(2,1)S(1)}, u32[]{:S(2)}, u32[]{:S(2)}) async-start(bf16[8,8,256]{2,0,1:T(8,128)(2,1)} %bitcast.122), calls=%async_computation.9 | async-start | bytes 65536 | tf_op jit(solution)/shard_map/all_to_all | solution.py:75
  1047.3 97.5 %all-reduce.24.cloned.1.call-start = ((), (), s32[]{:S(2)}) async-start(), calls=%async_computation.13 | async-start | bytes 1048576
  1064.7 139.2 %copy-start.13 = (f32[2048]{0:T(1024)S(1)}, f32[2048]{0:T(1024)}, u32[]{:S(2)}) copy-start(f32[2048]{0:T(1024)} %copy-done.11) | copy-start | bytes 24580
  1064.7 139.2 %copy-start.16 = (f32[2048]{0:T(1024)S(1)}, f32[2048]{0:T(1024)}, u32[]{:S(2)}) copy-start(f32[2048]{0:T(1024)} %copy-done.14) | copy-start | bytes 24580
  1064.7 139.2 %copy-start.31 = (f32[2048]{0:T(1024)S(1)}, f32[2048]{0:T(1024)}, u32[]{:S(2)}) copy-start(f32[2048]{0:T(1024)} %copy-done.30) | copy-start | bytes 24580
  1064.7 139.2 %copy-start.37 = (f32[2048]{0:T(1024)S(1)}, f32[2048]{0:T(1024)}, u32[]{:S(2)}) copy-start(f32[2048]{0:T(1024)} %copy-done.36) | copy-start | bytes 24580
  (30 other events, 977.1 us)
Sparse Core Ops, SparseCore 0:
  371.5 83.6 all-reduce.17
  604.7 78.4 all-reduce.19
  839.0 78.4 all-reduce.21
  1066.0 78.6 all-reduce.23
where the time goes:
time: 1230 us; the launch traced here: 1210 us
  blocking collectives  644 us (52%)
  waiting for transfers between devices  234 us (19%)
  starting transfers between devices  143 us (12%)
  other arithmetic  84.5 us (7%)
  local copies, waits for them, and re-layouts  59.6 us (5%)
  matrix products  31.3 us (3%)
  between operations  15.5 us (1%)
    psum x7, blocking collectives, normalize(): lax.psum((jnp.sum(states, axis=0), jnp.sum(states * states, axis=0)), 'fe...  410 us
    unnamed x8, waiting for transfers between devices  213 us
    all_gather x7, blocking collectives, forward_branch(): full_act = lax.all_gather(activ, 'feat', axis=0, tiled=True)  117 us
    all_to_all x4, starting transfers between devices, fetch_rim(): lax.all_to_all(outgoing, 'nodes', split_axis=1, concat_axis=1, tiled=True)  84.1 us
    all_to_all x4, starting transfers between devices, backward_branch(): lax.all_to_all(rim, 'nodes', split_axis=1, concat_axis=1, tiled=True)  59.4 us
    psum x1, blocking collectives, backward_branch(): lax.psum((jnp.sum(grad_norm, axis=0), jnp.sum(grad_norm * normed, axis=0)...  58.3 us
    scatter-add x4, other arithmetic, backward_branch(): source[:, :rows].at[:, send_index].add(returned).astype(jnp.bfloat16)  48.1 us
    gather x6, local copies, waits for them, and re-layouts, forward_branch(): jnp.take(mixed, send_index, axis=1)  39.7 us
  transfers between devices with their start and end apart: 12, of which 9 were waited for; matrix products, arithmetic and copies ran while one was open for 3% of the time, Pallas kernels for 0%

commit v1 on v0

v1 whole, which is shorter than its diff:
```python
import functools

import jax
import jax.numpy as jnp
from jax import lax
from jax.experimental import pallas as pl
from jax.experimental.pallas import tpu as pltpu
from jax.sharding import PartitionSpec as P

MESH = pl.DeviceIdType.MESH
TILE = 128
EPS = 1e-05
F32 = jnp.float32
BF16 = jnp.bfloat16


def dot(a, b):
    return jnp.dot(a, b, preferred_element_type=F32)


def dot_nt(a, b):
    return lax.dot_general(a, b, (((1,), (1,)), ((), ())), preferred_element_type=F32)


def kernel(
    n_nodes, n_feat,
    states_ref, grads_ref, weights_ref, adj_ref, rows_ref,
    source_ref, count_ref, sent_ref, order_ref, keep_ref, last_ref,
    out_ref, sg_ref, wg_ref,
    ag_send, ag_recv, x1, x2, g1, g2, wt,
    fwd_tiles, adj_sorted, pick, spread,
    normed, dgate, activ, inverse, mixed,
    src0, src1, src2, src3, halo_send, low, segs, rim_send, rim_recv, gm, gml,
    gw_send, gw_recv,
    ag_ss, ag_rs, h_ss, h_rs, r_ss, r_rs, w_ss, w_rs,
):
    src = (src0, src1, src2, src3)
    me_q = lax.axis_index("nodes")
    me_f = lax.axis_index("feat")
    width = states_ref.shape[1]
    rows = states_ref.shape[2]
    total = width * n_feat
    half = rows // 2
    blocks = rows // TILE
    chunks = rows // 256
    depth = adj_ref.shape[1]
    slots = blocks * depth

    def node_peer(d):
        return lax.rem(me_q + d, n_nodes)

    def feat_peer(d):
        return lax.rem(me_f + d, n_feat)

    barrier = pltpu.get_barrier_semaphore()
    for d in range(1, n_feat):
        pl.semaphore_signal(barrier, inc=1, device_id=(me_q, feat_peer(d)), device_id_type=MESH)
    for d in range(1, n_nodes):
        pl.semaphore_signal(barrier, inc=1, device_id=(node_peer(d), me_f), device_id_type=MESH)

    gathered = [(states_ref, 1, x2), (states_ref, 0, x1), (grads_ref, 1, g2), (grads_ref, 0, g1)]
    for a, (ref, group, _) in enumerate(gathered):
        packed = jnp.concatenate([ref[group, :, :half], ref[group, :, half:]], axis=0).astype(BF16)
        ag_send[a] = packed
        ag_recv[a, me_f] = packed
    pl.semaphore_wait(barrier, n_feat - 1 + n_nodes - 1)

    for a in range(len(gathered)):
        for d in range(1, n_feat):
            pltpu.make_async_remote_copy(
                src_ref=ag_send.at[a], dst_ref=ag_recv.at[a, me_f],
                send_sem=ag_ss.at[a], recv_sem=ag_rs.at[a],
                device_id=(me_q, feat_peer(d)), device_id_type=MESH,
            ).start()

    for layer in range(2):
        for group in range(2):
            wt[layer, group] = weights_ref[layer, group].astype(F32).T.astype(BF16)

    def prepare_block(t, _):
        for k in range(depth):
            keep = (k < count_ref[t]).astype(F32)
            tile = adj_ref[t, k].astype(F32) * keep
            fwd_tiles[t, k * TILE:(k + 1) * TILE, :] = tile.T.astype(BF16)
        return 0

    lax.fori_loop(0, blocks, prepare_block, 0)

    def prepare_sorted(i, _):
        e = order_ref[i]
        t = lax.div(e, depth)
        k = lax.rem(e, depth)
        keep = (k < count_ref[t]).astype(F32)
        adj_sorted[i] = (adj_ref[t, k].astype(F32) * keep).astype(BF16)
        return 0

    lax.fori_loop(0, slots, prepare_sorted, 0)

    def prepare_pick(p, _):
        lane = lax.broadcasted_iota(jnp.int32, (1, 256), 1)
        index = jnp.where(lane < sent_ref[0, p], rows_ref[0, pl.ds(p, 1), :], -1)
        high = lax.broadcasted_iota(jnp.int32, (256, 256), 0)
        for c in range(chunks):
            hit = high + c * 256 == index
            pick[p, c * 256:(c + 1) * 256, :] = jnp.where(hit, 1.0, 0.0).astype(BF16)
        value = index.astype(F32)
        place = lax.broadcasted_iota(jnp.int32, (TILE, 256), 1).astype(F32)
        for s in range(2):
            column = jnp.broadcast_to(value[:, s * TILE:(s + 1) * TILE], (TILE, TILE)).T
            column = jnp.concatenate([column, column], axis=1)
            for c in range(chunks):
                hit = place + float(c * 256) == column
                spread[p, s * TILE:(s + 1) * TILE, c * 256:(c + 1) * 256] = jnp.where(hit, 1.0, 0.0).astype(BF16)
        return 0

    lax.fori_loop(0, n_nodes, prepare_pick, 0)

    def take_gathered(a):
        ref, group, target = gathered[a]
        pltpu.make_async_remote_copy(
            src_ref=ag_recv.at[a, pl.ds(0, n_feat - 1)], dst_ref=ag_recv.at[a, pl.ds(0, n_feat - 1)],
            send_sem=ag_ss.at[a], recv_sem=ag_rs.at[a],
            device_id=(me_q, feat_peer(1)), device_id_type=MESH,
        ).wait_recv()
        for f in range(n_feat):
            got = ag_recv[a, f].astype(F32)
            target[f * width:(f + 1) * width, :half] = got[:width]
            target[f * width:(f + 1) * width, half:] = got[width:]
        target[pl.ds(pl.multiple_of(me_f * width, width), width), :] = ref[group]

    def lanes(c, size=256):
        return pl.ds(pl.multiple_of(c * size, size), size)

    def activate(u, b, with_gate):
        def step(c, _):
            states = u[:, lanes(c)]
            center = jnp.sum(states, axis=0, keepdims=True) * (1.0 / total)
            square = jnp.sum(states * states, axis=0, keepdims=True) * (1.0 / total)
            inv = lax.rsqrt(square - center * center + EPS)
            norm = (states - center) * inv
            gate = 1.0 / (1.0 + jnp.exp(-norm))
            normed[b, :, lanes(c)] = norm
            inverse[b, :, lanes(c)] = inv
            activ[b, :, lanes(c)] = (norm * gate).astype(BF16)
            if with_gate:
                dgate[b, :, lanes(c)] = gate * (1.0 + norm * (1.0 - gate))
            return 0

        lax.fori_loop(0, chunks, step, 0)

    def gates(b):
        def step(c, _):
            norm = normed[b, :, lanes(c)]
            gate = 1.0 / (1.0 + jnp.exp(-norm))
            dgate[b, :, lanes(c)] = gate * (1.0 + norm * (1.0 - gate))
            return 0

        lax.fori_loop(0, chunks, step, 0)

    def mix_and_send(b, layer, group):
        def step(c, _):
            value = dot(wt[layer, group], activ[b, :, lanes(c)]).astype(BF16)
            mixed[:, lanes(c)] = value
            src[b][2 * c] = value[:, :TILE]
            src[b][2 * c + 1] = value[:, TILE:]
            return 0

        lax.fori_loop(0, chunks, step, 0)

        def gather(p):
            return dot(mixed[...], pick[p]).astype(BF16)

        def send(i, _):
            p = node_peer(jnp.where(i < 7, i + 1, 0))
            value = gather(p)
            halo_send[b, p, 0] = value[:, :TILE]
            halo_send[b, p, 1] = value[:, TILE:]
            pltpu.make_async_remote_copy(
                src_ref=halo_send.at[b, p], dst_ref=src[b].at[pl.ds(blocks + 2 * me_q, 2)],
                send_sem=h_ss.at[b], recv_sem=h_rs.at[b],
                device_id=(p, me_f), device_id_type=MESH,
            ).start()
            return 0

        lax.fori_loop(0, n_nodes - 1, send, 0)
        value = gather(me_q)
        src[b][blocks + 2 * me_q] = value[:, :TILE]
        src[b][blocks + 2 * me_q + 1] = value[:, TILE:]

    def halo_wait(b):
        here = src[b].at[pl.ds(blocks, 2 * (n_nodes - 1))]
        pltpu.make_async_remote_copy(
            src_ref=here, dst_ref=here, send_sem=h_ss.at[b], recv_sem=h_rs.at[b],
            device_id=(node_peer(1), me_f), device_id_type=MESH,
        ).wait_recv()

    def aggregate(b, u):
        def step(t, _):
            tiles = [src[b][source_ref[t, k]] for k in range(depth)]
            u[:, lanes(t, TILE)] += dot(jnp.concatenate(tiles, axis=1), fwd_tiles[t])
            return 0

        lax.fori_loop(0, blocks, step, 0)

    def rims_and_send(b, g):
        def lower(t, _):
            low[t] = g[:, lanes(t, TILE)].astype(BF16)
            return 0

        lax.fori_loop(0, blocks, lower, 0)

        segs[0] = jnp.zeros((total, TILE), F32)

        def term(i, _):
            part = dot(low[lax.div(order_ref[i], depth)], adj_sorted[i])
            segs[i + 1] = part + keep_ref[i] * segs[i]
            return 0

        lax.fori_loop(0, slots, term, 0, unroll=4)

        def rim_tile(j):
            return segs[last_ref[j]].astype(BF16)

        def send(i, _):
            p = node_peer(i + 1)
            for s in range(2):
                rim_send[b, p, s] = rim_tile(blocks + 2 * p + s)
            pltpu.make_async_remote_copy(
                src_ref=rim_send.at[b, p], dst_ref=rim_recv.at[b, me_q],
                send_sem=r_ss.at[b], recv_sem=r_rs.at[b],
                device_id=(p, me_f), device_id_type=MESH,
            ).start()
            return 0

        lax.fori_loop(0, n_nodes - 1, send, 0)
        for s in range(2):
            rim_recv[b, me_q, s] = rim_tile(blocks + 2 * me_q + s)

        def local(t, _):
            gm[:, lanes(t, TILE)] = segs[last_ref[t]]
            return 0

        lax.fori_loop(0, blocks, local, 0)

    def rim_wait(b):
        here = rim_recv.at[b, pl.ds(0, n_nodes - 1)]
        pltpu.make_async_remote_copy(
            src_ref=here, dst_ref=here, send_sem=r_ss.at[b], recv_sem=r_rs.at[b],
            device_id=(node_peer(1), me_f), device_id_type=MESH,
        ).wait_recv()

    def scatter(b):
        def step(c, _):
            acc = gm[:, lanes(c)]
            for p in range(n_nodes):
                value = jnp.concatenate([rim_recv[b, p, 0], rim_recv[b, p, 1]], axis=1)
                acc = acc + dot(value, spread[p, :, lanes(c)])
            gm[:, lanes(c)] = acc
            gml[b, :, lanes(c)] = acc.astype(BF16)
            return 0

        lax.fori_loop(0, chunks, step, 0)

    def pull_back(b, layer, group, g):
        def step(c, _):
            gnorm = dot(weights_ref[layer, group], gml[b, :, lanes(c)]) * dgate[b, :, lanes(c)]
            norm = normed[b, :, lanes(c)]
            first = jnp.sum(gnorm, axis=0, keepdims=True) * (1.0 / total)
            second = jnp.sum(gnorm * norm, axis=0, keepdims=True) * (1.0 / total)
            g[:, lanes(c)] += inverse[b, :, lanes(c)] * (gnorm - first - norm * second)
            return 0

        lax.fori_loop(0, chunks, step, 0)

    def weight_send(b):
        mine = gm[pl.ds(pl.multiple_of(me_f * width, width), width), :].astype(BF16)
        part = dot_nt(mine, activ[b])
        gw_send[b] = part
        gw_recv[b, me_q] = part
        for d in range(1, n_nodes):
            pltpu.make_async_remote_copy(
                src_ref=gw_send.at[b], dst_ref=gw_recv.at[b, me_q],
                send_sem=w_ss.at[b], recv_sem=w_rs.at[b],
                device_id=(node_peer(d), me_f), device_id_type=MESH,
            ).start()

    def mine(ref):
        return ref[pl.ds(pl.multiple_of(me_f * width, width), width), :]

    take_gathered(0)
    activate(x2, 0, False)
    mix_and_send(0, 0, 0)
    take_gathered(1)
    gates(0)
    halo_wait(0)
    aggregate(0, x1)

    activate(x1, 1, False)
    mix_and_send(1, 0, 1)
    take_gathered(2)
    take_gathered(3)
    gates(1)
    rims_and_send(3, g2)
    halo_wait(1)
    aggregate(1, x2)

    activate(x2, 2, False)
    mix_and_send(2, 1, 0)
    gates(2)
    rim_wait(3)
    scatter(3)
    halo_wait(2)
    aggregate(2, x1)

    activate(x1, 3, True)
    out_ref[0] = mine(x1)
    pull_back(3, 1, 1, g1)
    weight_send(3)

    rims_and_send(2, g1)
    mix_and_send(3, 1, 1)
    rim_wait(2)
    scatter(2)
    pull_back(2, 1, 0, g2)
    weight_send(2)

    rims_and_send(1, g2)
    halo_wait(3)
    aggregate(3, x2)
    out_ref[1] = mine(x2)
    rim_wait(1)
    scatter(1)
    pull_back(1, 0, 1, g1)
    weight_send(1)

    rims_and_send(0, g1)
    sg_ref[0] = mine(g1)
    rim_wait(0)
    scatter(0)
    weight_send(0)
    pull_back(0, 0, 0, g2)
    sg_ref[1] = mine(g2)

    for b in range(4):
        here = gw_recv.at[b, pl.ds(0, n_nodes - 1)]
        pltpu.make_async_remote_copy(
            src_ref=here, dst_ref=here, send_sem=w_ss.at[b], recv_sem=w_rs.at[b],
            device_id=(node_peer(1), me_f), device_id_type=MESH,
        ).wait()
        summed = gw_recv[b, 0]
        for p in range(1, n_nodes):
            summed = summed + gw_recv[b, p]
        wg_ref[b // 2, b % 2] = summed
        here = src[b].at[pl.ds(blocks, 2 * (n_nodes - 1))]
        pltpu.make_async_remote_copy(
            src_ref=here, dst_ref=here, send_sem=h_ss.at[b], recv_sem=h_rs.at[b],
            device_id=(node_peer(1), me_f), device_id_type=MESH,
        ).wait_send()
        here = rim_recv.at[b, pl.ds(0, n_nodes - 1)]
        pltpu.make_async_remote_copy(
            src_ref=here, dst_ref=here, send_sem=r_ss.at[b], recv_sem=r_rs.at[b],
            device_id=(node_peer(1), me_f), device_id_type=MESH,
        ).wait_send()
        here = ag_recv.at[b, pl.ds(0, n_feat - 1)]
        pltpu.make_async_remote_copy(
            src_ref=here, dst_ref=here, send_sem=ag_ss.at[b], recv_sem=ag_rs.at[b],
            device_id=(me_q, feat_peer(1)), device_id_type=MESH,
        ).wait_send()


def sorted_slots(tile_source, source_tiles):
    source = tile_source.reshape(-1)
    n = source.shape[0]
    place = jnp.arange(n, dtype=jnp.int32)
    key = source * n + place
    rank = jnp.sum((key[None, :] < key[:, None]).astype(jnp.int32), axis=1)
    at = rank[None, :] == place[:, None]
    order = jnp.sum(jnp.where(at, place[None, :], 0), axis=1)
    ordered = jnp.sum(jnp.where(at, source[None, :], 0), axis=1)
    keep = jnp.concatenate([jnp.zeros((1,), F32), (ordered[1:] == ordered[:-1]).astype(F32)])
    tiles = jnp.arange(source_tiles, dtype=jnp.int32)
    upto = jnp.sum((source[None, :] <= tiles[:, None]).astype(jnp.int32), axis=1)
    has = jnp.any(source[None, :] == tiles[:, None], axis=1)
    return order, keep, jnp.where(has, upto, 0)


def solution(mesh):
    n_nodes, n_feat = mesh.shape["nodes"], mesh.shape["feat"]

    def body(node_states, weights, adj_tiles, tile_source, tile_count, send_rows, send_count, out_grads):
        groups, width, rows = node_states.shape
        total = width * n_feat
        blocks, depth = tile_source.shape
        slots = send_rows.shape[2]
        source_tiles = blocks + n_nodes * slots // TILE
        order, keep, last = sorted_slots(tile_source, source_tiles)
        vmem = pl.BlockSpec(memory_space=pltpu.VMEM)
        smem = pl.BlockSpec(memory_space=pltpu.SMEM)
        dma = pltpu.SemaphoreType.DMA((4,))
        outs = pl.pallas_call(
            functools.partial(kernel, n_nodes, n_feat),
            out_shape=(
                jax.ShapeDtypeStruct(node_states.shape, F32),
                jax.ShapeDtypeStruct(out_grads.shape, F32),
                jax.ShapeDtypeStruct((2, 2, width, total), F32),
            ),
            in_specs=[vmem] * 5 + [smem] * 6,
            out_specs=(vmem, vmem, vmem),
            scratch_shapes=[
                pltpu.VMEM((4, 2 * width, rows // 2), BF16),
                pltpu.VMEM((4, n_feat, 2 * width, rows // 2), BF16),
                pltpu.VMEM((total, rows), F32),
                pltpu.VMEM((total, rows), F32),
                pltpu.VMEM((total, rows), F32),
                pltpu.VMEM((total, rows), F32),
                pltpu.VMEM((2, 2, total, total), BF16),
                pltpu.VMEM((blocks, depth * TILE, TILE), BF16),
                pltpu.VMEM((blocks * depth, TILE, TILE), BF16),
                pltpu.VMEM((n_nodes, rows, slots), BF16),
                pltpu.VMEM((n_nodes, slots, rows), BF16),
                pltpu.VMEM((4, total, rows), F32),
                pltpu.VMEM((4, total, rows), F32),
                pltpu.VMEM((4, total, rows), BF16),
                pltpu.VMEM((4, 1, rows), F32),
                pltpu.VMEM((total, rows), BF16),
                *[pltpu.VMEM((source_tiles, total, TILE), BF16)] * 4,
                pltpu.VMEM((4, n_nodes, 2, total, TILE), BF16),
                pltpu.VMEM((blocks, total, TILE), BF16),
                pltpu.VMEM((blocks * depth + 1, total, TILE), F32),
                pltpu.VMEM((4, n_nodes, 2, total, TILE), BF16),
                pltpu.VMEM((4, n_nodes, 2, total, TILE), BF16),
                pltpu.VMEM((total, rows), F32),
                pltpu.VMEM((4, total, rows), BF16),
                pltpu.VMEM((4, width, total), F32),
                pltpu.VMEM((4, n_nodes, width, total), F32),
                dma, dma, dma, dma, dma, dma, dma, dma,
            ],
            compiler_params=pltpu.CompilerParams(
                collective_id=0, has_side_effects=True, vmem_limit_bytes=62 * 2**20
            ),
        )(
            node_states, out_grads, weights, adj_tiles, send_rows,
            tile_source, tile_count, send_count, order, keep, last,
        )
        return outs[0], outs[1], jnp.swapaxes(outs[2], 2, 3)

    return jax.shard_map(
        body,
        mesh=mesh,
        in_specs=(
            P(None, "feat", "nodes"),
            P(),
            P("nodes", None, None, None),
            P("nodes", None),
            P("nodes"),
            P("nodes", None, None),
            P("nodes", None),
            P(None, "feat", "nodes"),
        ),
        out_specs=(P(None, "feat", "nodes"), P(None, "feat", "nodes"), P(None, None, None, "feat")),
        check_vma=False,
    )
```

time: 1230 us -> 122 us (0.10); the launches traced: 1210 us -> 122 us
  blocking collectives: 644 us -> 0 us
  waiting for transfers between devices: 234 us -> 0 us
  starting transfers between devices: 143 us -> 0 us
  Pallas kernels: 0 us -> 114 us
  other arithmetic: 84.5 us -> 2.26 us
  local copies, waits for them, and re-layouts: 59.6 us -> 5.31 us
  matrix products: 31.3 us -> 0 us
  between operations: 15.5 us -> 0.66 us
    psum x9 -> x0, blocking collectives: 494 us -> none  [the longest x7 410 us: normalize(): lax.psum((jnp.sum(states, axis=0), jnp.sum(states * states, axis=0)), 'fe...]
    unnamed x8 -> x0, waiting for transfers between devices: 213 us -> none
    all_to_all x8 -> x0, starting transfers between devices: 143 us -> none  [the longest x4 84.1 us: fetch_rim(): lax.all_to_all(outgoing, 'nodes', split_axis=1, concat_axis=1, tiled=True)]
    all_gather x7 -> x0, blocking collectives: 117 us -> none  [forward_branch(): full_act = lax.all_gather(activ, 'feat', axis=0, tiled=True)]
    pallas_call x0 -> x1, Pallas kernels: none -> 114 us  [body(): pl.pallas_call(functools.partial(kernel, n_nodes, n_feat), out_shape=(jax...]
    scatter-add x8 -> x0, other arithmetic: 59.1 us -> none  [the longest x4 48.1 us: backward_branch(): source[:, :rows].at[:, send_index].add(returned).astype(jnp.bfloat16)]
    gather x12 -> x0, local copies, waits for them, and re-layouts: 43.4 us -> none  [the longest x6 39.7 us: forward_branch(): jnp.take(mixed, send_index, axis=1)]
    all_to_all x2 -> x0, blocking collectives: 33.2 us -> none  [fetch_rim(): lax.all_to_all(outgoing, 'nodes', split_axis=1, concat_axis=1, tiled=True)]
  transfers between devices with their start and end apart: 12 -> 0, of which waited for: 9 -> 0; matrix products, arithmetic and copies ran while one was open for 3% -> 0% of each run, Pallas kernels for 0% -> 0%
where the time goes in v1:
time: 122 us
  Pallas kernels  114 us (93%)
  local copies, waits for them, and re-layouts  5.31 us (4%)
  other arithmetic  2.26 us (2%)
    pallas_call x1, Pallas kernels, body(): pl.pallas_call(functools.partial(kernel, n_nodes, n_feat), out_shape=(jax...  114 us
    unnamed x6, local copies, waits for them, and re-layouts  5.22 us

profile of v1, /device:TPU:1, one launch (start us, length us, event | category | flops | bytes accessed | tf_op | source)
XLA Modules:
  0.0 122.0 jit_solution(2217358713313400608)
XLA Ops:
  0.6 0.8 copy.16.source_ref
  1.4 0.0 copy-start
  1.4 0.1 reshape.29
  1.5 0.1 convert_reduce_fusion.1
  1.6 0.1 fusion
  1.7 0.5 broadcast_select_fusion.last_ref
  2.3 0.2 convert_reduce_fusion
  2.4 0.6 select_reduce_fusion
  3.1 0.1 slice_compare_fusion
  3.2 0.6 add_convert_fusion.keep_ref
  3.7 0.0 copy-done
  3.7 113.8 %shard_map.103 = (f32[2,8,2048]{2,1,0:T(8,128)}, f32[2,8,2048]{2,1,0:T(8,128)}, f32[2,2,8,128]{3,2,1,0:T(8,128)}) custom-call(f32[2,8,2048]{2,1,0:T(8,128)} %states_ref.1, f32[2,8,2048]{2,1,0:T(8,128)} %grads_ref.1, bf16[2,2,128,128]{3,2,1,0:T(8,128)(2,1)} %weights_ref.1, bf16[16,4,128,128]{3,2,1,0:T(8,128)(2,1)} %adj_ref.1, s32[1,8,256]{2,1,0:T(8,128)} %rows_ref.1, ...), custom_call_target="tpu_custom_call" | custom-call | tf_op jit(solution)/shard_map/pallas_call | solution.py:400
  117.5 1.6 %copy.20 = f32[2,8,2048]{2,1,0:T(8,128)} copy(f32[2,8,2048]{2,1,0:T(8,128)} %get-tuple-element.14) | data formatting | bytes 262144
  119.1 1.6 %copy.21 = f32[2,8,2048]{2,1,0:T(8,128)} copy(f32[2,8,2048]{2,1,0:T(8,128)} %get-tuple-element.15) | data formatting | bytes 262144
  120.7 1.3 %copy.22 = f32[2,2,128,8]{2,3,1,0:T(8,128)} copy(f32[2,2,128,8]{2,3,1,0:T(8,128)} %bitcast.1) | data formatting | bytes 32768
  (1 shorter events, 0.0 us)
Async XLA Ops:
  1.4 2.4 %copy-start = (s32[16,4]{1,0:T(8,128)}, s32[16,4]{1,0:T(8,128)S(1)}, u32[]{:S(2)}) copy-start(s32[16,4]{1,0:T(8,128)S(1)} %copy.16.source_ref) | copy-start | bytes 772

commit v2 on v1

v2 whole, which is shorter than its diff:
```python
import functools

import jax
import jax.numpy as jnp
from jax import lax
from jax.experimental import pallas as pl
from jax.experimental.pallas import tpu as pltpu
from jax.sharding import PartitionSpec as P

MESH = pl.DeviceIdType.MESH
TILE = 128
EPS = 1e-05
TERM_UNROLL = 8
F32 = jnp.float32
BF16 = jnp.bfloat16


def dot(a, b):
    return jnp.dot(a, b, preferred_element_type=F32)


def dot_nt(a, b):
    return lax.dot_general(a, b, (((1,), (1,)), ((), ())), preferred_element_type=F32)


def kernel(
    n_nodes, n_feat,
    states_ref, grads_ref, weights_ref, adj_hbm, rows_ref,
    source_ref, count_ref, sent_ref,
    out_ref, sg_ref, wg_ref,
    adj_ref, plan_rows, plan, local_sems,
    ag_send, ag_recv, x1, x2, g1, g2, wt,
    fwd_tiles, adj_sorted, pick, spread,
    normed, dgate, activ, inverse, mixed,
    src0, src1, src2, src3, halo_out, low, segs, rim_out, rim_in, gm, gml,
    gw_send, gw_recv,
    ag_ss, ag_rs, h_ss, h_rs, r_ss, r_rs, w_ss, w_rs,
):
    src = (src0, src1, src2, src3)
    me_q = lax.axis_index("nodes")
    me_f = lax.axis_index("feat")
    width = states_ref.shape[1]
    rows = states_ref.shape[2]
    total = width * n_feat
    half = rows // 2
    blocks = rows // TILE
    chunks = rows // 256
    depth = adj_ref.shape[1]
    slots = blocks * depth
    adj_copy = pltpu.make_async_copy(adj_hbm, adj_ref, local_sems.at[0])
    adj_copy.start()

    me_x, me_c = lax.div(me_q, 2), lax.rem(me_q, 2)
    me_z, me_y = lax.div(me_f, 4), lax.rem(me_f, 4)

    def node_peer(shift):
        dx, dc = shift
        return lax.rem(me_x + dx, n_nodes // 2) * 2 + lax.rem(me_c + dc, 2)

    def feat_peer(shift):
        dz, dy = shift
        return lax.rem(me_z + dz, n_feat // 4) * 4 + lax.rem(me_y + dy, 4)

    def hops(shift):
        return min(shift[0], 4 - shift[0]) + min(shift[1], 4 - shift[1])

    feat_shifts = [(dz, dy) for dz in range(4) for dy in range(4) if dz or dy]
    feat_shifts.sort(key=lambda shift: -hops(shift))
    mate = (0, 1)
    groups = [((2, 0), (2, 1)), ((1, 0), (3, 0)), ((1, 1), (3, 1))]
    far_shifts = [shift for group in groups for shift in group]
    node_shifts = far_shifts + [mate]

    def back(shift):
        return ((4 - shift[0]) % 4, shift[1])

    started = []
    barrier = pltpu.get_barrier_semaphore()
    for shift in feat_shifts:
        pl.semaphore_signal(barrier, inc=1, device_id=(me_q, feat_peer(shift)), device_id_type=MESH)
    for shift in node_shifts:
        pl.semaphore_signal(barrier, inc=1, device_id=(node_peer(shift), me_f), device_id_type=MESH)

    gathered = [(states_ref, 1, x2), (states_ref, 0, x1), (grads_ref, 1, g2), (grads_ref, 0, g1)]
    for a, (ref, group, _) in enumerate(gathered):
        packed = jnp.concatenate([ref[group, :, :half], ref[group, :, half:]], axis=0).astype(BF16)
        ag_send[a] = packed
        ag_recv[a, me_f] = packed
    for layer in range(2):
        for group in range(2):
            wt[layer, group] = weights_ref[layer, group].astype(F32).T.astype(BF16)

    lane = lax.broadcasted_iota(jnp.int32, (1, TILE), 1)
    source = jnp.full((1, TILE), blocks * TILE, jnp.int32)
    for e in range(slots):
        source = jnp.where(lane == e, source_ref[e // blocks, e % blocks], source)
    place = lax.broadcasted_iota(jnp.int32, (TILE, TILE), 0)
    lanes_of = lax.broadcasted_iota(jnp.int32, (TILE, TILE), 1)

    def column(row):
        return jnp.broadcast_to(row, (TILE, TILE)).T

    source_column = column(source)
    key = source * TILE + lane
    rank = column(jnp.sum((column(key) < key).astype(jnp.int32), axis=0, keepdims=True))
    at = rank == lanes_of
    before = rank + 1 == lanes_of
    order = jnp.sum(jnp.where(at, place, 0), axis=0, keepdims=True)
    ordered = jnp.sum(jnp.where(at, source_column, 0), axis=0, keepdims=True)
    previous = jnp.sum(jnp.where(before, source_column, 0), axis=0, keepdims=True)
    keep = jnp.where((ordered == previous) & (lane > 0), 1, 0)
    upto = jnp.sum((source_column <= lanes_of).astype(jnp.int32), axis=0, keepdims=True)
    has = jnp.sum((source_column == lanes_of).astype(jnp.int32), axis=0, keepdims=True)
    plan_rows[0:1, :] = order
    plan_rows[1:2, :] = keep
    plan_rows[2:3, :] = jnp.where(has > 0, upto, 0)
    plan_copy = pltpu.make_async_copy(plan_rows, plan, local_sems.at[1])
    plan_copy.start()

    def prepare_block(t, _):
        for k in range(depth):
            keep = (k < count_ref[t]).astype(F32)
            tile = adj_ref[t, k].astype(F32) * keep
            fwd_tiles[t, k * TILE:(k + 1) * TILE, :] = tile.T.astype(BF16)
        return 0

    adj_copy.wait()
    lax.fori_loop(0, blocks, prepare_block, 0)

    def prepare_sorted(i, _):
        e = plan[0, i]
        t = lax.rem(e, blocks)
        k = lax.div(e, blocks)
        keep = (k < count_ref[t]).astype(F32)
        adj_sorted[i] = (adj_ref[t, k].astype(F32) * keep).astype(BF16)
        return 0

    plan_copy.wait()
    lax.fori_loop(0, slots, prepare_sorted, 0)

    def prepare_pick(p, _):
        lane = lax.broadcasted_iota(jnp.int32, (1, 256), 1)
        index = jnp.where(lane < sent_ref[0, p], rows_ref[0, pl.ds(p, 1), :], -1)
        high = lax.broadcasted_iota(jnp.int32, (256, 256), 0)
        for c in range(chunks):
            hit = high + c * 256 == index
            pick[p, c * 256:(c + 1) * 256, :] = jnp.where(hit, 1.0, 0.0).astype(BF16)
        value = index.astype(F32)
        place = lax.broadcasted_iota(jnp.int32, (TILE, 256), 1).astype(F32)
        for s in range(2):
            column = jnp.broadcast_to(value[:, s * TILE:(s + 1) * TILE], (TILE, TILE)).T
            column = jnp.concatenate([column, column], axis=1)
            for c in range(chunks):
                hit = place + float(c * 256) == column
                spread[p, s * TILE:(s + 1) * TILE, c * 256:(c + 1) * 256] = jnp.where(hit, 1.0, 0.0).astype(BF16)
        return 0

    lax.fori_loop(0, n_nodes, prepare_pick, 0)

    pl.semaphore_wait(barrier, n_feat - 1 + n_nodes - 1)

    def send_gathered(a):
        for shift in feat_shifts:
            pltpu.make_async_remote_copy(
                src_ref=ag_send.at[a], dst_ref=ag_recv.at[a, me_f],
                send_sem=ag_ss.at[a], recv_sem=ag_rs.at[a],
                device_id=(me_q, feat_peer(shift)), device_id_type=MESH,
            ).start()

    send_gathered(0)
    send_gathered(1)

    def take_gathered(a):
        ref, group, target = gathered[a]
        pltpu.make_async_remote_copy(
            src_ref=ag_recv.at[a, pl.ds(0, n_feat - 1)], dst_ref=ag_recv.at[a, pl.ds(0, n_feat - 1)],
            send_sem=ag_ss.at[a], recv_sem=ag_rs.at[a],
            device_id=(me_q, feat_peer((0, 1))), device_id_type=MESH,
        ).wait_recv()
        for f in range(n_feat):
            got = ag_recv[a, f].astype(F32)
            target[f * width:(f + 1) * width, :half] = got[:width]
            target[f * width:(f + 1) * width, half:] = got[width:]
        target[pl.ds(pl.multiple_of(me_f * width, width), width), :] = ref[group]

    def lanes(c, size=256):
        return pl.ds(pl.multiple_of(c * size, size), size)

    def copy_to_node(source, target, sends, receives, shift):
        return pltpu.make_async_remote_copy(
            src_ref=source, dst_ref=target, send_sem=sends, recv_sem=receives,
            device_id=(node_peer(shift), me_f), device_id_type=MESH,
        )

    def forward(b, layer, group, u, add=None, with_gate=False):
        def step(c, _):
            states = u[:, lanes(c)]
            if add is not None:
                parts = []
                for h in range(2):
                    tiles = [src[add][source_ref[k, 2 * c + h]] for k in range(depth)]
                    parts.append(dot(jnp.concatenate(tiles, axis=1), fwd_tiles[2 * c + h]))
                states = states + jnp.concatenate(parts, axis=1)
                u[:, lanes(c)] = states
            center = jnp.sum(states, axis=0, keepdims=True) * (1.0 / total)
            square = jnp.sum(states * states, axis=0, keepdims=True) * (1.0 / total)
            inv = lax.rsqrt(square - center * center + EPS)
            norm = (states - center) * inv
            gate = 1.0 / (1.0 + jnp.exp(-norm))
            normed[b, :, lanes(c)] = norm
            inverse[b, :, lanes(c)] = inv
            act = (norm * gate).astype(BF16)
            activ[b, :, lanes(c)] = act
            if with_gate:
                dgate[b, :, lanes(c)] = gate * (1.0 + norm * (1.0 - gate))
            value = dot(wt[layer, group], act).astype(BF16)
            mixed[:, lanes(c)] = value
            src[b][2 * c] = value[:, :TILE]
            src[b][2 * c + 1] = value[:, TILE:]
            return 0

        lax.fori_loop(0, chunks, step, 0, unroll=2)

    def aggregate(b, u):
        def step(t, _):
            tiles = [src[b][source_ref[k, t]] for k in range(depth)]
            u[:, lanes(t, TILE)] += dot(jnp.concatenate(tiles, axis=1), fwd_tiles[t])
            return 0

        lax.fori_loop(0, blocks, step, 0, unroll=4)

    def gates(b):
        def step(c, _):
            norm = normed[b, :, lanes(c)]
            gate = 1.0 / (1.0 + jnp.exp(-norm))
            dgate[b, :, lanes(c)] = gate * (1.0 + norm * (1.0 - gate))
            return 0

        lax.fori_loop(0, chunks, step, 0)

    def halo_send(b):
        for shift in node_shifts:
            p = node_peer(shift)
            value = dot(mixed[...], pick[p]).astype(BF16)
            halo_out[b, p, 0] = value[:, :TILE]
            halo_out[b, p, 1] = value[:, TILE:]
            copy_to_node(
                halo_out.at[b, p], src[b].at[pl.ds(blocks + 2 * me_q, 2)], h_ss.at[b], h_rs.at[b], shift
            ).start()
        started.append((h_ss.at[b], src[b].at[pl.ds(blocks, 2 * (n_nodes - 1))]))
        value = dot(mixed[...], pick[me_q]).astype(BF16)
        src[b][blocks + 2 * me_q] = value[:, :TILE]
        src[b][blocks + 2 * me_q + 1] = value[:, TILE:]

    def halo_wait(b):
        here = src[b].at[pl.ds(blocks, 2 * (n_nodes - 1))]
        copy_to_node(here, here, h_ss.at[b], h_rs.at[b], mate).wait_recv()

    def lower(g):
        def step(t, _):
            low[t] = g[:, lanes(t, TILE)].astype(BF16)
            return 0

        lax.fori_loop(0, blocks, step, 0)

    def terms():
        segs[0] = jnp.zeros((total, TILE), F32)

        def step(j, _):
            acc = segs[TERM_UNROLL * j]
            for n in range(TERM_UNROLL):
                i = TERM_UNROLL * j + n
                part = dot(low[lax.rem(plan[0, i], blocks)], adj_sorted[i])
                acc = part + plan[1, i].astype(F32) * acc
                segs[i + 1] = acc
            return 0

        lax.fori_loop(0, slots // TERM_UNROLL, step, 0)

    def rim_send(b):
        def rim(p):
            tiles = [segs[plan[2, blocks + 2 * p + s]] for s in range(2)]
            return jnp.concatenate(tiles, axis=1).astype(BF16)

        for n, shift in enumerate([mate] + far_shifts):
            p = node_peer(shift)
            rim_out[b, p] = rim(p)
            copy_to_node(
                rim_out.at[b, p], rim_in.at[b, me_q], r_ss.at[b], r_rs.at[b, (n + 1) // 2], shift
            ).start()
        started.append((r_ss.at[b], rim_in.at[b, pl.ds(0, n_nodes - 1)]))
        own = rim(me_q)

        def local(c, _):
            tiles = [segs[plan[2, 2 * c + h]] for h in range(2)]
            gm[:, lanes(c)] = jnp.concatenate(tiles, axis=1) + dot(own, spread[me_q, :, lanes(c)])
            return 0

        lax.fori_loop(0, chunks, local, 0, unroll=2)

    def rim_wait(b, n):
        here = rim_in.at[b, pl.ds(0, 1 if n == 0 else 2)]
        copy_to_node(here, here, r_ss.at[b], r_rs.at[b, n], mate).wait_recv()

    def rim_add(b, n):
        rim_wait(b, n)
        peers = [node_peer(back(shift)) for shift in ([mate] if n == 0 else groups[n - 1])]

        def step(c, _):
            acc = gm[:, lanes(c)]
            for p in peers:
                acc = acc + dot(rim_in[b, p], spread[p, :, lanes(c)])
            gm[:, lanes(c)] = acc
            return 0

        lax.fori_loop(0, chunks, step, 0, unroll=2)

    def pull_back(b, layer, group, g, last=True):
        if last:
            rim_wait(b, 3)
            peers = [node_peer(back(shift)) for shift in groups[2]]

        def step(c, _):
            acc = gm[:, lanes(c)]
            if last:
                for p in peers:
                    acc = acc + dot(rim_in[b, p], spread[p, :, lanes(c)])
            value = acc.astype(BF16)
            gml[:, lanes(c)] = value
            gnorm = dot(weights_ref[layer, group], value) * dgate[b, :, lanes(c)]
            norm = normed[b, :, lanes(c)]
            first = jnp.sum(gnorm, axis=0, keepdims=True) * (1.0 / total)
            second = jnp.sum(gnorm * norm, axis=0, keepdims=True) * (1.0 / total)
            state = g[:, lanes(c)] + inverse[b, :, lanes(c)] * (gnorm - first - norm * second)
            g[:, lanes(c)] = state
            state = state.astype(BF16)
            low[2 * c] = state[:, :TILE]
            low[2 * c + 1] = state[:, TILE:]
            return 0

        lax.fori_loop(0, chunks, step, 0, unroll=2)

    def weight_send(b):
        own = gml[pl.ds(pl.multiple_of(lax.div(me_f, 2) * 2 * width, 2 * width), 2 * width), :]
        part = dot_nt(own, activ[b])
        part = jnp.where(lax.rem(me_f, 2) == 0, part[:width], part[width:])
        gw_send[b] = part
        gw_recv[b, me_q] = part
        for shift in node_shifts:
            copy_to_node(gw_send.at[b], gw_recv.at[b, me_q], w_ss.at[b], w_rs.at[b], shift).start()

    def mine(ref):
        return ref[pl.ds(pl.multiple_of(me_f * width, width), width), :]

    take_gathered(0)
    forward(0, 0, 0, x2)
    halo_send(0)
    send_gathered(2)
    take_gathered(1)
    gates(0)
    halo_wait(0)

    forward(1, 0, 1, x1, add=0)
    halo_send(1)
    send_gathered(3)
    gates(1)
    take_gathered(2)
    lower(g2)
    terms()
    rim_send(3)
    halo_wait(1)

    forward(2, 1, 0, x2, add=1)
    halo_send(2)
    gates(2)
    take_gathered(3)
    rim_add(3, 0)
    rim_add(3, 1)
    rim_add(3, 2)
    rim_add(3, 3)
    halo_wait(2)

    forward(3, 1, 1, x1, add=2, with_gate=True)
    pull_back(3, 1, 1, g1, last=False)
    terms()
    rim_send(2)
    weight_send(3)
    halo_send(3)
    out_ref[0] = mine(x1)
    rim_add(2, 0)
    rim_add(2, 1)
    rim_add(2, 2)
    pull_back(2, 1, 0, g2)

    terms()
    rim_send(1)
    weight_send(2)
    halo_wait(3)
    aggregate(3, x2)
    out_ref[1] = mine(x2)
    rim_add(1, 0)
    rim_add(1, 1)
    rim_add(1, 2)
    pull_back(1, 0, 1, g1)

    terms()
    rim_send(0)
    weight_send(1)
    sg_ref[0] = mine(g1)
    rim_add(0, 0)
    rim_add(0, 1)
    rim_add(0, 2)
    pull_back(0, 0, 0, g2)
    weight_send(0)
    sg_ref[1] = mine(g2)

    for b in range(4):
        here = gw_recv.at[b, pl.ds(0, n_nodes - 1)]
        pltpu.make_async_remote_copy(
            src_ref=here, dst_ref=here, send_sem=w_ss.at[b], recv_sem=w_rs.at[b],
            device_id=(node_peer(mate), me_f), device_id_type=MESH,
        ).wait()
        summed = gw_recv[b, 0]
        for p in range(1, n_nodes):
            summed = summed + gw_recv[b, p]
        wg_ref[b // 2, b % 2] = summed
        here = ag_recv.at[b, pl.ds(0, n_feat - 1)]
        pltpu.make_async_remote_copy(
            src_ref=here, dst_ref=here, send_sem=ag_ss.at[b], recv_sem=ag_rs.at[b],
            device_id=(me_q, feat_peer((0, 1))), device_id_type=MESH,
        ).wait_send()
    for sends, here in started:
        copy_to_node(here, here, sends, h_rs.at[0], mate).wait_send()


def hand_over(out, sg, wg, out_ref, sg_ref, wg_ref):
    out_ref[...] = out[...]
    sg_ref[...] = sg[...]
    wg_ref[...] = wg[...]


def solution(mesh):
    n_nodes, n_feat = mesh.shape["nodes"], mesh.shape["feat"]

    def body(node_states, weights, adj_tiles, tile_source, tile_count, send_rows, send_count, out_grads):
        groups, width, rows = node_states.shape
        total = width * n_feat
        blocks, depth = tile_source.shape
        slots = send_rows.shape[2]
        source_tiles = blocks + n_nodes * slots // TILE
        vmem = pl.BlockSpec(memory_space=pltpu.VMEM)
        smem = pl.BlockSpec(memory_space=pltpu.SMEM)
        dma = pltpu.SemaphoreType.DMA((4,))
        outs = pl.pallas_call(
            functools.partial(kernel, n_nodes, n_feat),
            out_shape=(
                jax.ShapeDtypeStruct(node_states.shape, F32),
                jax.ShapeDtypeStruct(out_grads.shape, F32),
                jax.ShapeDtypeStruct((2, 2, width, total), F32),
            ),
            in_specs=[vmem, vmem, vmem, pl.BlockSpec(memory_space=pl.ANY), vmem, smem, smem, smem],
            out_specs=(vmem, vmem, vmem),
            scratch_shapes=[
                pltpu.VMEM(adj_tiles.shape, BF16),
                pltpu.VMEM((8, TILE), jnp.int32),
                pltpu.SMEM((8, TILE), jnp.int32),
                pltpu.SemaphoreType.DMA((2,)),
                pltpu.VMEM((4, 2 * width, rows // 2), BF16),
                pltpu.VMEM((4, n_feat, 2 * width, rows // 2), BF16),
                pltpu.VMEM((total, rows), F32),
                pltpu.VMEM((total, rows), F32),
                pltpu.VMEM((total, rows), F32),
                pltpu.VMEM((total, rows), F32),
                pltpu.VMEM((2, 2, total, total), BF16),
                pltpu.VMEM((blocks, depth * TILE, TILE), BF16),
                pltpu.VMEM((blocks * depth, TILE, TILE), BF16),
                pltpu.VMEM((n_nodes, rows, slots), BF16),
                pltpu.VMEM((n_nodes, slots, rows), BF16),
                pltpu.VMEM((4, total, rows), F32),
                pltpu.VMEM((4, total, rows), F32),
                pltpu.VMEM((4, total, rows), BF16),
                pltpu.VMEM((4, 1, rows), F32),
                pltpu.VMEM((total, rows), BF16),
                *[pltpu.VMEM((source_tiles, total, TILE), BF16)] * 4,
                pltpu.VMEM((4, n_nodes, 2, total, TILE), BF16),
                pltpu.VMEM((blocks, total, TILE), BF16),
                pltpu.VMEM((blocks * depth + 1, total, TILE), F32),
                pltpu.VMEM((4, n_nodes, total, slots), BF16),
                pltpu.VMEM((4, n_nodes, total, slots), BF16),
                pltpu.VMEM((total, rows), F32),
                pltpu.VMEM((total, rows), BF16),
                pltpu.VMEM((4, width, total), F32),
                pltpu.VMEM((4, n_nodes, width, total), F32),
                dma, dma, dma, dma, dma, pltpu.SemaphoreType.DMA((4, 4)), dma, dma,
            ],
            compiler_params=pltpu.CompilerParams(
                collective_id=0, has_side_effects=True, vmem_limit_bytes=62 * 2**20
            ),
        )(
            node_states, out_grads, weights, adj_tiles, send_rows,
            tile_source.T, tile_count, send_count,
        )
        outs = pl.pallas_call(
            hand_over,
            out_shape=tuple(jax.ShapeDtypeStruct(o.shape, o.dtype) for o in outs),
            in_specs=[vmem] * 3,
            out_specs=(vmem,) * 3,
        )(*outs)
        return outs[0], outs[1], jnp.swapaxes(outs[2], 2, 3)

    return jax.shard_map(
        body,
        mesh=mesh,
        in_specs=(
            P(None, "feat", "nodes"),
            P(),
            P("nodes", None, None, None),
            P("nodes", None),
            P("nodes"),
            P("nodes", None, None),
            P("nodes", None),
            P(None, "feat", "nodes"),
        ),
        out_specs=(P(None, "feat", "nodes"), P(None, "feat", "nodes"), P(None, None, None, "feat")),
        check_vma=False,
    )
```

time: 122 us -> 105 us (0.86); the launches traced: 122 us -> 104 us
  Pallas kernels: 114 us -> 103 us
  local copies, waits for them, and re-layouts: 5.31 us -> 0 us
  other arithmetic: 2.26 us -> 0 us
    pallas_call x1, Pallas kernels: 114 us -> 101 us  [body(): pl.pallas_call(functools.partial(kernel, n_nodes, n_feat), out_shape=(jax...]
    unnamed x6 -> x0, local copies, waits for them, and re-layouts: 5.22 us -> none
    pallas_call x0 -> x1, Pallas kernels: none -> 1.68 us  [body(): pl.pallas_call(hand_over, out_shape=tuple((jax.ShapeDtypeStruct(o.shape,...]
where the time goes in v2:
time: 105 us; the launch traced here: 104 us
  Pallas kernels  103 us (98%)
    pallas_call x1, Pallas kernels, body(): pl.pallas_call(functools.partial(kernel, n_nodes, n_feat), out_shape=(jax...  101 us

profile of v2, /device:TPU:1, one launch (start us, length us, event | category | flops | bytes accessed | tf_op | source)
XLA Modules:
  0.0 103.8 jit_solution(1111382370006979353)
XLA Ops:
  0.6 101.5 %shard_map.103 = (f32[2,8,2048]{2,1,0:T(8,128)}, f32[2,8,2048]{2,1,0:T(8,128)}, f32[2,2,8,128]{3,2,1,0:T(8,128)}) custom-call(f32[2,8,2048]{2,1,0:T(8,128)} %states_ref.1, f32[2,8,2048]{2,1,0:T(8,128)} %grads_ref.1, bf16[2,2,128,128]{3,2,1,0:T(8,128)(2,1)} %weights_ref.1, bf16[16,4,128,128]{3,2,1,0:T(8,128)(2,1)} %adj_hbm.1, s32[1,8,256]{2,1,0:T(8,128)} %rows_ref.1, ...), custom_call_target="tpu_custom_call" | custom-call | tf_op jit(solution)/shard_map/pallas_call | solution.py:454
  102.1 1.7 %shard_map.104 = (f32[2,8,2048]{2,1,0:T(8,128)}, f32[2,8,2048]{2,1,0:T(8,128)}, f32[2,2,8,128]{3,2,1,0:T(8,128)}) custom-call(f32[2,8,2048]{2,1,0:T(8,128)} %get-tuple-element.9.out, f32[2,8,2048]{2,1,0:T(8,128)} %get-tuple-element.10.sg, f32[2,2,8,128]{3,2,1,0:T(8,128)} %get-tuple-element.11.wg), custom_call_target="tpu_custom_call" | custom-call | tf_op jit(solution)/shard_map/pallas_call | solution.py:503

commit v3 on v2

--- a/solution.py
+++ b/solution.py
@@ -25,16 +25,17 @@
 
 def kernel(
     n_nodes, n_feat,
-    states_ref, grads_ref, weights_ref, adj_hbm, rows_ref,
+    states_hbm, grads_hbm, weights_hbm, adj_hbm, rows_hbm,
     source_ref, count_ref, sent_ref,
-    out_ref, sg_ref, wg_ref,
+    out_hbm, sg_hbm, wg_hbm,
+    states_ref, grads_ref, weights_ref, rows_ref, out_ref, sg_ref, wg_ref,
     adj_ref, plan_rows, plan, local_sems,
-    ag_send, ag_recv, x1, x2, g1, g2, wt,
+    ag_send, ag_recv, line_send, line_recv, line_ss, line_rs, x1, x2, g1, g2, wt,
     fwd_tiles, adj_sorted, pick, spread,
     normed, dgate, activ, inverse, mixed,
     src0, src1, src2, src3, halo_out, low, segs, rim_out, rim_in, gm, gml,
-    gw_send, gw_recv,
-    ag_ss, ag_rs, h_ss, h_rs, r_ss, r_rs, w_ss, w_rs,
+    gw_send, gw_recv, own_in, gml16, out_sems,
+    ag_ss, ag_rs, h_ss, h_rs, r_ss, r_rs, w_ss, w_rs, own_sems,
 ):
     src = (src0, src1, src2, src3)
     me_q = lax.axis_index("nodes")
@@ -47,8 +48,6 @@
     chunks = rows // 256
     depth = adj_ref.shape[1]
     slots = blocks * depth
-    adj_copy = pltpu.make_async_copy(adj_hbm, adj_ref, local_sems.at[0])
-    adj_copy.start()
 
     me_x, me_c = lax.div(me_q, 2), lax.rem(me_q, 2)
     me_z, me_y = lax.div(me_f, 4), lax.rem(me_f, 4)
@@ -75,17 +74,36 @@
         return ((4 - shift[0]) % 4, shift[1])
 
     started = []
+    started_feat = []
     barrier = pltpu.get_barrier_semaphore()
     for shift in feat_shifts:
         pl.semaphore_signal(barrier, inc=1, device_id=(me_q, feat_peer(shift)), device_id_type=MESH)
     for shift in node_shifts:
         pl.semaphore_signal(barrier, inc=1, device_id=(node_peer(shift), me_f), device_id_type=MESH)
 
+    states_copy = pltpu.make_async_copy(states_hbm, states_ref, local_sems.at[2])
+    grads_copy = pltpu.make_async_copy(grads_hbm, grads_ref, local_sems.at[3])
+    rows_copy = pltpu.make_async_copy(rows_hbm, rows_ref, local_sems.at[4])
+    weights_copy = pltpu.make_async_copy(weights_hbm, weights_ref, local_sems.at[5])
+    adj_copy = pltpu.make_async_copy(adj_hbm, adj_ref, local_sems.at[0])
+    for copy in (states_copy, grads_copy, rows_copy, weights_copy, adj_copy):
+        copy.start()
+    states_copy.wait()
+    grads_copy.wait()
+
     gathered = [(states_ref, 1, x2), (states_ref, 0, x1), (grads_ref, 1, g2), (grads_ref, 0, g1)]
     for a, (ref, group, _) in enumerate(gathered):
         packed = jnp.concatenate([ref[group, :, :half], ref[group, :, half:]], axis=0).astype(BF16)
-        ag_send[a] = packed
-        ag_recv[a, me_f] = packed
+        if a == 0:
+            ag_send[...] = packed
+            ag_recv[me_f] = packed
+        else:
+            quarter = half // 2
+            line_send[a - 1, 0] = packed[:, :quarter]
+            line_send[a - 1, 1] = packed[:, quarter:]
+            line_recv[a - 1, 0, me_z, me_y] = packed[:, :quarter]
+            line_recv[a - 1, 1, me_y, me_z] = packed[:, quarter:]
+    weights_copy.wait()
     for layer in range(2):
         for group in range(2):
             wt[layer, group] = weights_ref[layer, group].astype(F32).T.astype(BF16)
@@ -155,32 +173,71 @@
                 spread[p, s * TILE:(s + 1) * TILE, c * 256:(c + 1) * 256] = jnp.where(hit, 1.0, 0.0).astype(BF16)
         return 0
 
+    rows_copy.wait()
     lax.fori_loop(0, n_nodes, prepare_pick, 0)
 
     pl.semaphore_wait(barrier, n_feat - 1 + n_nodes - 1)
 
-    def send_gathered(a):
+    def copy_to_feat(source, target, sends, receives, shift):
+        return pltpu.make_async_remote_copy(
+            src_ref=source, dst_ref=target, send_sem=sends, recv_sem=receives,
+            device_id=(me_q, feat_peer(shift)), device_id_type=MESH,
+        )
+
+    lines = ([(0, 2), (0, 1), (0, 3)], [(2, 0), (1, 0), (3, 0)])
+    place_of = ((me_z, me_y), (me_y, me_z))
+
+    def send_direct():
         for shift in feat_shifts:
-            pltpu.make_async_remote_copy(
-                src_ref=ag_send.at[a], dst_ref=ag_recv.at[a, me_f],
-                send_sem=ag_ss.at[a], recv_sem=ag_rs.at[a],
-                device_id=(me_q, feat_peer(shift)), device_id_type=MESH,
-            ).start()
-
-    send_gathered(0)
-    send_gathered(1)
+            copy_to_feat(ag_send, ag_recv.at[me_f], ag_ss.at[0], ag_rs.at[0], shift).start()
+        started_feat.append((ag_ss.at[0], ag_recv.at[pl.ds(0, n_feat - 1)]))
+
+    def send_lines(a):
+        for w in range(2):
+            first, second = place_of[w]
+            for shift in lines[w]:
+                copy_to_feat(
+                    line_send.at[a - 1, w], line_recv.at[a - 1, w, first, second],
+                    line_ss.at[a, w], line_rs.at[a, w], shift,
+                ).start()
+            started_feat.append((line_ss.at[a, w], line_recv.at[a - 1, w, 0, pl.ds(0, 3)]))
+
+    def relay_lines(a):
+        for w in range(2):
+            here = line_recv.at[a - 1, w, 0, pl.ds(0, 3)]
+            copy_to_feat(here, here, line_ss.at[a, w], line_rs.at[a, w], (0, 1)).wait_recv()
+            first = place_of[w][0]
+            for shift in lines[1 - w]:
+                copy_to_feat(
+                    line_recv.at[a - 1, w, first], line_recv.at[a - 1, w, first],
+                    line_ss.at[a, 2 + w], line_rs.at[a, 2 + w], shift,
+                ).start()
+            started_feat.append((line_ss.at[a, 2 + w], line_recv.at[a - 1, w, pl.ds(0, 3)]))
+
+    send_direct()
+    for a in range(1, 4):
+        send_lines(a)
 
     def take_gathered(a):
         ref, group, target = gathered[a]
-        pltpu.make_async_remote_copy(
-            src_ref=ag_recv.at[a, pl.ds(0, n_feat - 1)], dst_ref=ag_recv.at[a, pl.ds(0, n_feat - 1)],
-            send_sem=ag_ss.at[a], recv_sem=ag_rs.at[a],
-            device_id=(me_q, feat_peer((0, 1))), device_id_type=MESH,
-        ).wait_recv()
-        for f in range(n_feat):
-            got = ag_recv[a, f].astype(F32)
-            target[f * width:(f + 1) * width, :half] = got[:width]
-            target[f * width:(f + 1) * width, half:] = got[width:]
+        if a == 0:
+            here = ag_recv.at[pl.ds(0, n_feat - 1)]
+            copy_to_feat(here, here, ag_ss.at[0], ag_rs.at[0], (0, 1)).wait_recv()
+            for f in range(n_feat):
+                got = ag_recv[f].astype(F32)
+                target[f * width:(f + 1) * width, :half] = got[:width]
+                target[f * width:(f + 1) * width, half:] = got[width:]
+        else:
+            quarter = half // 2
+            for w in range(2):
+                here = line_recv.at[a - 1, w, pl.ds(0, 3)]
+                copy_to_feat(here, here, line_ss.at[a, 2 + w], line_rs.at[a, 2 + w], (0, 1)).wait_recv()
+                for f in range(n_feat):
+                    z, y = f // 4, f % 4
+                    got = line_recv[a - 1, w, (z, y)[w], (y, z)[w]].astype(F32)
+                    at = w * quarter
+                    target[f * width:(f + 1) * width, at:at + quarter] = got[:width]
+                    target[f * width:(f + 1) * width, half + at:half + at + quarter] = got[width:]
         target[pl.ds(pl.multiple_of(me_f * width, width), width), :] = ref[group]
 
     def lanes(c, size=256):
@@ -192,16 +249,9 @@
             device_id=(node_peer(shift), me_f), device_id_type=MESH,
         )
 
-    def forward(b, layer, group, u, add=None, with_gate=False):
+    def forward(b, layer, group, u, with_gate=False):
         def step(c, _):
             states = u[:, lanes(c)]
-            if add is not None:
-                parts = []
-                for h in range(2):
-                    tiles = [src[add][source_ref[k, 2 * c + h]] for k in range(depth)]
-                    parts.append(dot(jnp.concatenate(tiles, axis=1), fwd_tiles[2 * c + h]))
-                states = states + jnp.concatenate(parts, axis=1)
-                u[:, lanes(c)] = states
             center = jnp.sum(states, axis=0, keepdims=True) * (1.0 / total)
             square = jnp.sum(states * states, axis=0, keepdims=True) * (1.0 / total)
             inv = lax.rsqrt(square - center * center + EPS)
@@ -239,22 +289,23 @@
         lax.fori_loop(0, chunks, step, 0)
 
     def halo_send(b):
-        for shift in node_shifts:
+        for n, shift in enumerate(node_shifts):
             p = node_peer(shift)
             value = dot(mixed[...], pick[p]).astype(BF16)
             halo_out[b, p, 0] = value[:, :TILE]
             halo_out[b, p, 1] = value[:, TILE:]
             copy_to_node(
-                halo_out.at[b, p], src[b].at[pl.ds(blocks + 2 * me_q, 2)], h_ss.at[b], h_rs.at[b], shift
+                halo_out.at[b, p], src[b].at[pl.ds(blocks + 2 * me_q, 2)], h_ss.at[b], h_rs.at[b, n // 2], shift
             ).start()
         started.append((h_ss.at[b], src[b].at[pl.ds(blocks, 2 * (n_nodes - 1))]))
         value = dot(mixed[...], pick[me_q]).astype(BF16)
         src[b][blocks + 2 * me_q] = value[:, :TILE]
         src[b][blocks + 2 * me_q + 1] = value[:, TILE:]
 
-    def halo_wait(b):
-        here = src[b].at[pl.ds(blocks, 2 * (n_nodes - 1))]
-        copy_to_node(here, here, h_ss.at[b], h_rs.at[b], mate).wait_recv()
+    def halo_wait(b, parts=range(4)):
+        for n in parts:
+            here = src[b].at[pl.ds(blocks, 2 if n == 3 else 4)]
+            copy_to_node(here, here, h_ss.at[b], h_rs.at[b, n], mate).wait_recv()
 
     def lower(g):
         def step(t, _):
@@ -277,17 +328,24 @@
 
         lax.fori_loop(0, slots // TERM_UNROLL, step, 0)
 
-    def rim_send(b):
+    def rim_send(b, early_rows=False):
         def rim(p):
             tiles = [segs[plan[2, blocks + 2 * p + s]] for s in range(2)]
             return jnp.concatenate(tiles, axis=1).astype(BF16)
 
-        for n, shift in enumerate([mate] + far_shifts):
+        rows16 = pl.ds(pl.multiple_of(lax.div(me_f, 2) * 2 * width, 2 * width), 2 * width)
+        for n, shift in enumerate(node_shifts):
             p = node_peer(shift)
             rim_out[b, p] = rim(p)
+            if early_rows:
+                copy_to_node(rim_out.at[b, p, rows16], own_in.at[me_q], own_sems.at[0], own_sems.at[1], shift).start()
+        for n, shift in enumerate(node_shifts):
+            p = node_peer(shift)
             copy_to_node(
-                rim_out.at[b, p], rim_in.at[b, me_q], r_ss.at[b], r_rs.at[b, (n + 1) // 2], shift
+                rim_out.at[b, p], rim_in.at[b, me_q], r_ss.at[b], r_rs.at[b, n // 2], shift
             ).start()
+        if early_rows:
+            started.append((own_sems.at[0], own_in.at[pl.ds(0, n_nodes - 1)]))
         started.append((r_ss.at[b], rim_in.at[b, pl.ds(0, n_nodes - 1)]))
         own = rim(me_q)
 
@@ -299,12 +357,12 @@
         lax.fori_loop(0, chunks, local, 0, unroll=2)
 
     def rim_wait(b, n):
-        here = rim_in.at[b, pl.ds(0, 1 if n == 0 else 2)]
+        here = rim_in.at[b, pl.ds(0, 1 if n == 3 else 2)]
         copy_to_node(here, here, r_ss.at[b], r_rs.at[b, n], mate).wait_recv()
 
     def rim_add(b, n):
         rim_wait(b, n)
-        peers = [node_peer(back(shift)) for shift in ([mate] if n == 0 else groups[n - 1])]
+        peers = [node_peer(back(shift)) for shift in ([mate] if n == 3 else groups[n])]
 
         def step(c, _):
             acc = gm[:, lanes(c)]
@@ -317,7 +375,7 @@
 
     def pull_back(b, layer, group, g, last=True):
         if last:
-            rim_wait(b, 3)
+            rim_wait(b, 2)
             peers = [node_peer(back(shift)) for shift in groups[2]]
 
         def step(c, _):
@@ -340,8 +398,32 @@
 
         lax.fori_loop(0, chunks, step, 0, unroll=2)
 
-    def weight_send(b):
-        own = gml[pl.ds(pl.multiple_of(lax.div(me_f, 2) * 2 * width, 2 * width), 2 * width), :]
+    puts = []
+
+    def put(source, target, n):
+        copy = pltpu.make_async_copy(source, target, out_sems.at[n])
+        copy.start()
+        puts.append(copy)
+
+    def early_weight_rows():
+        here = own_in.at[pl.ds(0, n_nodes - 1)]
+        copy_to_node(here, here, own_sems.at[0], own_sems.at[1], mate).wait_recv()
+        rows16 = pl.ds(pl.multiple_of(lax.div(me_f, 2) * 2 * width, 2 * width), 2 * width)
+        peers = [node_peer(shift) for shift in node_shifts]
+
+        def step(c, _):
+            acc = gm[rows16, lanes(c)]
+            for p in peers:
+                acc = acc + dot(own_in[p], spread[p, :, lanes(c)])
+            gml16[:, lanes(c)] = acc.astype(BF16)
+            return 0
+
+        lax.fori_loop(0, chunks, step, 0, unroll=2)
+        weight_send(0, gml16[...])
+
+    def weight_send(b, own=None):
+        if own is None:
+            own = gml[pl.ds(pl.multiple_of(lax.div(me_f, 2) * 2 * width, 2 * width), 2 * width), :]
         part = dot_nt(own, activ[b])
         part = jnp.where(lax.rem(me_f, 2) == 0, part[:width], part[width:])
         gw_send[b] = part
@@ -355,41 +437,46 @@
     take_gathered(0)
     forward(0, 0, 0, x2)
     halo_send(0)
-    send_gathered(2)
+    relay_lines(1)
+    relay_lines(2)
+    relay_lines(3)
+    gates(0)
     take_gathered(1)
-    gates(0)
     halo_wait(0)
-
-    forward(1, 0, 1, x1, add=0)
+    aggregate(0, x1)
+
+    forward(1, 0, 1, x1)
     halo_send(1)
-    send_gathered(3)
     gates(1)
     take_gathered(2)
     lower(g2)
     terms()
     rim_send(3)
     halo_wait(1)
-
-    forward(2, 1, 0, x2, add=1)
+    aggregate(1, x2)
+
+    forward(2, 1, 0, x2)
     halo_send(2)
     gates(2)
     take_gathered(3)
+    rim_add(3, 3)
     rim_add(3, 0)
     rim_add(3, 1)
     rim_add(3, 2)
-    rim_add(3, 3)
     halo_wait(2)
-
-    forward(3, 1, 1, x1, add=2, with_gate=True)
+    aggregate(2, x1)
+
+    forward(3, 1, 1, x1, with_gate=True)
     pull_back(3, 1, 1, g1, last=False)
     terms()
     rim_send(2)
     weight_send(3)
     halo_send(3)
     out_ref[0] = mine(x1)
+    put(out_ref.at[0], out_hbm.at[0], 0)
+    rim_add(2, 3)
     rim_add(2, 0)
     rim_add(2, 1)
-    rim_add(2, 2)
     pull_back(2, 1, 0, g2)
 
     terms()
@@ -398,21 +485,24 @@
     halo_wait(3)
     aggregate(3, x2)
     out_ref[1] = mine(x2)
+    put(out_ref.at[1], out_hbm.at[1], 1)
+    rim_add(1, 3)
     rim_add(1, 0)
     rim_add(1, 1)
-    rim_add(1, 2)
     pull_back(1, 0, 1, g1)
 
     terms()
-    rim_send(0)
+    rim_send(0, early_rows=True)
     weight_send(1)
     sg_ref[0] = mine(g1)
+    put(sg_ref.at[0], sg_hbm.at[0], 2)
+    early_weight_rows()
+    rim_add(0, 3)
     rim_add(0, 0)
     rim_add(0, 1)
-    rim_add(0, 2)
     pull_back(0, 0, 0, g2)
-    weight_send(0)
     sg_ref[1] = mine(g2)
+    put(sg_ref.at[1], sg_hbm.at[1], 3)
 
     for b in range(4):
         here = gw_recv.at[b, pl.ds(0, n_nodes - 1)]
@@ -424,13 +514,14 @@
         for p in range(1, n_nodes):
             summed = summed + gw_recv[b, p]
         wg_ref[b // 2, b % 2] = summed
-        here = ag_recv.at[b, pl.ds(0, n_feat - 1)]
-        pltpu.make_async_remote_copy(
-            src_ref=here, dst_ref=here, send_sem=ag_ss.at[b], recv_sem=ag_rs.at[b],
-            device_id=(me_q, feat_peer((0, 1))), device_id_type=MESH,
-        ).wait_send()
+        if b == 3:
+            put(wg_ref, wg_hbm, 4)
+    for sends, here in started_feat:
+        copy_to_feat(here, here, sends, ag_rs.at[0], (0, 1)).wait_send()
     for sends, here in started:
-        copy_to_node(here, here, sends, h_rs.at[0], mate).wait_send()
+        copy_to_node(here, here, sends, w_rs.at[0], mate).wait_send()
+    for copy in puts:
+        copy.wait()
 
 
 def hand_over(out, sg, wg, out_ref, sg_ref, wg_ref):
@@ -450,6 +541,7 @@
         source_tiles = blocks + n_nodes * slots // TILE
         vmem = pl.BlockSpec(memory_space=pltpu.VMEM)
         smem = pl.BlockSpec(memory_space=pltpu.SMEM)
+        hbm = pl.BlockSpec(memory_space=pl.ANY)
         dma = pltpu.SemaphoreType.DMA((4,))
         outs = pl.pallas_call(
             functools.partial(kernel, n_nodes, n_feat),
@@ -458,15 +550,26 @@
                 jax.ShapeDtypeStruct(out_grads.shape, F32),
                 jax.ShapeDtypeStruct((2, 2, width, total), F32),
             ),
-            in_specs=[vmem, vmem, vmem, pl.BlockSpec(memory_space=pl.ANY), vmem, smem, smem, smem],
-            out_specs=(vmem, vmem, vmem),
+            in_specs=[hbm] * 5 + [smem] * 3,
+            out_specs=(hbm,) * 3,
             scratch_shapes=[
+                pltpu.VMEM(node_states.shape, F32),
+                pltpu.VMEM(out_grads.shape, F32),
+                pltpu.VMEM(weights.shape, BF16),
+                pltpu.VMEM(send_rows.shape, jnp.int32),
+                pltpu.VMEM(node_states.shape, F32),
+                pltpu.VMEM(out_grads.shape, F32),
+                pltpu.VMEM((2, 2, width, total), F32),
                 pltpu.VMEM(adj_tiles.shape, BF16),
                 pltpu.VMEM((8, TILE), jnp.int32),
                 pltpu.SMEM((8, TILE), jnp.int32),
-                pltpu.SemaphoreType.DMA((2,)),
-                pltpu.VMEM((4, 2 * width, rows // 2), BF16),
-                pltpu.VMEM((4, n_feat, 2 * width, rows // 2), BF16),
+                pltpu.SemaphoreType.DMA((6,)),
+                pltpu.VMEM((2 * width, rows // 2), BF16),
+                pltpu.VMEM((n_feat, 2 * width, rows // 2), BF16),
+                pltpu.VMEM((3, 2, 2 * width, rows // 4), BF16),
+                pltpu.VMEM((3, 2, 4, n_feat // 4, 2 * width, rows // 4), BF16),
+                pltpu.SemaphoreType.DMA((4, 4)),
+                pltpu.SemaphoreType.DMA((4, 4)),
                 pltpu.VMEM((total, rows), F32),
                 pltpu.VMEM((total, rows), F32),
                 pltpu.VMEM((total, rows), F32),
@@ -491,7 +594,11 @@
                 pltpu.VMEM((total, rows), BF16),
                 pltpu.VMEM((4, width, total), F32),
                 pltpu.VMEM((4, n_nodes, width, total), F32),
-                dma, dma, dma, dma, dma, pltpu.SemaphoreType.DMA((4, 4)), dma, dma,
+                pltpu.VMEM((n_nodes, 2 * width, slots), BF16),
+                pltpu.VMEM((2 * width, rows), BF16),
+                pltpu.SemaphoreType.DMA((5,)),
+                dma, dma, dma, pltpu.SemaphoreType.DMA((4, 4)), dma, pltpu.SemaphoreType.DMA((4, 4)), dma, dma,
+                pltpu.SemaphoreType.DMA((2,)),
             ],
             compiler_params=pltpu.CompilerParams(
                 collective_id=0, has_side_effects=True, vmem_limit_bytes=62 * 2**20

time: 105 us -> 103 us (0.981)
    pallas_call x1, Pallas kernels: 101 us -> 100 us  [body(): pl.pallas_call(functools.partial(kernel, n_nodes, n_feat), out_shape=(jax...]
where the time goes in v3:
time: 103 us; the launch traced here: 102 us
  Pallas kernels  102 us (99%)
    pallas_call x1, Pallas kernels, body(): pl.pallas_call(functools.partial(kernel, n_nodes, n_feat), out_shape=(jax...  100 us

profile of v3, /device:TPU:1, one launch (start us, length us, event | category | flops | bytes accessed | tf_op | source)
XLA Modules:
  0.0 102.3 jit_solution(10941005093508881903)
XLA Ops:
  0.6 100.0 %shard_map.103 = (f32[2,8,2048]{2,1,0:T(8,128)}, f32[2,8,2048]{2,1,0:T(8,128)}, f32[2,2,8,128]{3,2,1,0:T(8,128)}) custom-call(f32[2,8,2048]{2,1,0:T(8,128)} %states_hbm.1, f32[2,8,2048]{2,1,0:T(8,128)} %grads_hbm.1, bf16[2,2,128,128]{3,2,1,0:T(8,128)(2,1)} %weights_hbm.1, bf16[16,4,128,128]{3,2,1,0:T(8,128)(2,1)} %adj_hbm.1, s32[1,8,256]{2,1,0:T(8,128)} %rows_hbm.1, ...), custom_call_target="tpu_custom_call" | custom-call | tf_op jit(solution)/shard_map/pallas_call | solution.py:546
  100.7 1.7 %shard_map.104 = (f32[2,8,2048]{2,1,0:T(8,128)}, f32[2,8,2048]{2,1,0:T(8,128)}, f32[2,2,8,128]{3,2,1,0:T(8,128)}) custom-call(f32[2,8,2048]{2,1,0:T(8,128)} %get-tuple-element.9.out, f32[2,8,2048]{2,1,0:T(8,128)} %get-tuple-element.10.sg, f32[2,2,8,128]{3,2,1,0:T(8,128)} %get-tuple-element.11.wg), custom_call_target="tpu_custom_call" | custom-call | tf_op jit(solution)/shard_map/pallas_call | solution.py:610

commit v4 on v3

--- a/solution.py
+++ b/solution.py
@@ -10,7 +10,7 @@
 MESH = pl.DeviceIdType.MESH
 TILE = 128
 EPS = 1e-05
-TERM_UNROLL = 8
+TERM_UNROLL = 32
 F32 = jnp.float32
 BF16 = jnp.bfloat16
 
@@ -269,7 +269,7 @@
             src[b][2 * c + 1] = value[:, TILE:]
             return 0
 
-        lax.fori_loop(0, chunks, step, 0, unroll=2)
+        lax.fori_loop(0, chunks, step, 0, unroll=8)
 
     def aggregate(b, u):
         def step(t, _):
@@ -277,7 +277,7 @@
             u[:, lanes(t, TILE)] += dot(jnp.concatenate(tiles, axis=1), fwd_tiles[t])
             return 0
 
-        lax.fori_loop(0, blocks, step, 0, unroll=4)
+        lax.fori_loop(0, blocks, step, 0, unroll=16)
 
     def gates(b):
         def step(c, _):
@@ -396,7 +396,7 @@
             low[2 * c + 1] = state[:, TILE:]
             return 0
 
-        lax.fori_loop(0, chunks, step, 0, unroll=2)
+        lax.fori_loop(0, chunks, step, 0, unroll=4)
 
     puts = []
 

time: 103 us -> 96.1 us (0.933)
  Pallas kernels: 102 us -> 95.3 us
    pallas_call x1, Pallas kernels: 100 us -> 93.6 us  [body(): pl.pallas_call(functools.partial(kernel, n_nodes, n_feat), out_shape=(jax...]
where the time goes in v4:
time: 96.1 us; the launch traced here: 95.9 us
  Pallas kernels  95.3 us (99%)
    pallas_call x1, Pallas kernels, body(): pl.pallas_call(functools.partial(kernel, n_nodes, n_feat), out_shape=(jax...  93.6 us

profile of v4, /device:TPU:1, one launch (start us, length us, event | category | flops | bytes accessed | tf_op | source)
XLA Modules:
  0.0 95.9 jit_solution(5019579665343852161)
XLA Ops:
  0.6 93.6 %shard_map.103 = (f32[2,8,2048]{2,1,0:T(8,128)}, f32[2,8,2048]{2,1,0:T(8,128)}, f32[2,2,8,128]{3,2,1,0:T(8,128)}) custom-call(f32[2,8,2048]{2,1,0:T(8,128)} %states_hbm.1, f32[2,8,2048]{2,1,0:T(8,128)} %grads_hbm.1, bf16[2,2,128,128]{3,2,1,0:T(8,128)(2,1)} %weights_hbm.1, bf16[16,4,128,128]{3,2,1,0:T(8,128)(2,1)} %adj_hbm.1, s32[1,8,256]{2,1,0:T(8,128)} %rows_hbm.1, ...), custom_call_target="tpu_custom_call" | custom-call | tf_op jit(solution)/shard_map/pallas_call | solution.py:546
  94.2 1.7 %shard_map.104 = (f32[2,8,2048]{2,1,0:T(8,128)}, f32[2,8,2048]{2,1,0:T(8,128)}, f32[2,2,8,128]{3,2,1,0:T(8,128)}) custom-call(f32[2,8,2048]{2,1,0:T(8,128)} %get-tuple-element.9.out, f32[2,8,2048]{2,1,0:T(8,128)} %get-tuple-element.10.sg, f32[2,2,8,128]{3,2,1,0:T(8,128)} %get-tuple-element.11.wg), custom_call_target="tpu_custom_call" | custom-call | tf_op jit(solution)/shard_map/pallas_call | solution.py:610

commit v5 on v4

--- a/solution.py
+++ b/solution.py
@@ -383,9 +383,13 @@
             if last:
                 for p in peers:
                     acc = acc + dot(rim_in[b, p], spread[p, :, lanes(c)])
-            value = acc.astype(BF16)
-            gml[:, lanes(c)] = value
-            gnorm = dot(weights_ref[layer, group], value) * dgate[b, :, lanes(c)]
+            gml[:, lanes(c)] = acc.astype(BF16)
+            return 0
+
+        lax.fori_loop(0, chunks, step, 0, unroll=4)
+
+        def second_step(c, _):
+            gnorm = dot(weights_ref[layer, group], gml[:, lanes(c)]) * dgate[b, :, lanes(c)]
             norm = normed[b, :, lanes(c)]
             first = jnp.sum(gnorm, axis=0, keepdims=True) * (1.0 / total)
             second = jnp.sum(gnorm * norm, axis=0, keepdims=True) * (1.0 / total)
@@ -396,7 +400,7 @@
             low[2 * c + 1] = state[:, TILE:]
             return 0
 
-        lax.fori_loop(0, chunks, step, 0, unroll=4)
+        lax.fori_loop(0, chunks, second_step, 0, unroll=8)
 
     puts = []
 

time: 96.1 us -> 94.6 us (0.984)
  Pallas kernels: 95.3 us -> 93.8 us
    pallas_call x1, Pallas kernels: 93.6 us -> 92.1 us  [body(): pl.pallas_call(functools.partial(kernel, n_nodes, n_feat), out_shape=(jax...]
where the time goes in v5:
time: 94.6 us; the launch traced here: 94.5 us
  Pallas kernels  93.8 us (99%)
    pallas_call x1, Pallas kernels, body(): pl.pallas_call(functools.partial(kernel, n_nodes, n_feat), out_shape=(jax...  92.1 us

profile of v5, /device:TPU:1, one launch (start us, length us, event | category | flops | bytes accessed | tf_op | source)
XLA Modules:
  0.0 94.5 jit_solution(5024740110932908764)
XLA Ops:
  0.6 92.1 %shard_map.103 = (f32[2,8,2048]{2,1,0:T(8,128)}, f32[2,8,2048]{2,1,0:T(8,128)}, f32[2,2,8,128]{3,2,1,0:T(8,128)}) custom-call(f32[2,8,2048]{2,1,0:T(8,128)} %states_hbm.1, f32[2,8,2048]{2,1,0:T(8,128)} %grads_hbm.1, bf16[2,2,128,128]{3,2,1,0:T(8,128)(2,1)} %weights_hbm.1, bf16[16,4,128,128]{3,2,1,0:T(8,128)(2,1)} %adj_hbm.1, s32[1,8,256]{2,1,0:T(8,128)} %rows_hbm.1, ...), custom_call_target="tpu_custom_call" | custom-call | tf_op jit(solution)/shard_map/pallas_call | solution.py:550
  92.8 1.7 %shard_map.104 = (f32[2,8,2048]{2,1,0:T(8,128)}, f32[2,8,2048]{2,1,0:T(8,128)}, f32[2,2,8,128]{3,2,1,0:T(8,128)}) custom-call(f32[2,8,2048]{2,1,0:T(8,128)} %get-tuple-element.9.out, f32[2,8,2048]{2,1,0:T(8,128)} %get-tuple-element.10.sg, f32[2,2,8,128]{3,2,1,0:T(8,128)} %get-tuple-element.11.wg), custom_call_target="tpu_custom_call" | custom-call | tf_op jit(solution)/shard_map/pallas_call | solution.py:614

commit v6 on v5

--- a/solution.py
+++ b/solution.py
@@ -354,7 +354,7 @@
             gm[:, lanes(c)] = jnp.concatenate(tiles, axis=1) + dot(own, spread[me_q, :, lanes(c)])
             return 0
 
-        lax.fori_loop(0, chunks, local, 0, unroll=2)
+        lax.fori_loop(0, chunks, local, 0, unroll=4)
 
     def rim_wait(b, n):
         here = rim_in.at[b, pl.ds(0, 1 if n == 3 else 2)]
@@ -371,7 +371,7 @@
             gm[:, lanes(c)] = acc
             return 0
 
-        lax.fori_loop(0, chunks, step, 0, unroll=2)
+        lax.fori_loop(0, chunks, step, 0, unroll=4)
 
     def pull_back(b, layer, group, g, last=True):
         if last:
@@ -422,7 +422,7 @@
             gml16[:, lanes(c)] = acc.astype(BF16)
             return 0
 
-        lax.fori_loop(0, chunks, step, 0, unroll=2)
+        lax.fori_loop(0, chunks, step, 0, unroll=4)
         weight_send(0, gml16[...])
 
     def weight_send(b, own=None):

time: 94.6 us -> 93.6 us (0.989)
  Pallas kernels: 93.8 us -> 92.7 us
    pallas_call x1, Pallas kernels: 92.1 us -> 91.1 us  [body(): pl.pallas_call(functools.partial(kernel, n_nodes, n_feat), out_shape=(jax...]
where the time goes in v6:
time: 93.6 us; the launch traced here: 93.4 us
  Pallas kernels  92.7 us (99%)
    pallas_call x1, Pallas kernels, body(): pl.pallas_call(functools.partial(kernel, n_nodes, n_feat), out_shape=(jax...  91.1 us

profile of v6, /device:TPU:1, one launch (start us, length us, event | category | flops | bytes accessed | tf_op | source)
XLA Modules:
  0.0 93.4 jit_solution(10782811622463904996)
XLA Ops:
  0.6 91.1 %shard_map.103 = (f32[2,8,2048]{2,1,0:T(8,128)}, f32[2,8,2048]{2,1,0:T(8,128)}, f32[2,2,8,128]{3,2,1,0:T(8,128)}) custom-call(f32[2,8,2048]{2,1,0:T(8,128)} %states_hbm.1, f32[2,8,2048]{2,1,0:T(8,128)} %grads_hbm.1, bf16[2,2,128,128]{3,2,1,0:T(8,128)(2,1)} %weights_hbm.1, bf16[16,4,128,128]{3,2,1,0:T(8,128)(2,1)} %adj_hbm.1, s32[1,8,256]{2,1,0:T(8,128)} %rows_hbm.1, ...), custom_call_target="tpu_custom_call" | custom-call | tf_op jit(solution)/shard_map/pallas_call | solution.py:550
  91.7 1.7 %shard_map.104 = (f32[2,8,2048]{2,1,0:T(8,128)}, f32[2,8,2048]{2,1,0:T(8,128)}, f32[2,2,8,128]{3,2,1,0:T(8,128)}) custom-call(f32[2,8,2048]{2,1,0:T(8,128)} %get-tuple-element.9.out, f32[2,8,2048]{2,1,0:T(8,128)} %get-tuple-element.10.sg, f32[2,2,8,128]{3,2,1,0:T(8,128)} %get-tuple-element.11.wg), custom_call_target="tpu_custom_call" | custom-call | tf_op jit(solution)/shard_map/pallas_call | solution.py:614
